TPU v7x, 32 devices: a whole 2x2x4 slice. The times are simulated.
32 devices in a mesh: grp: 4 (over y, x), tp: 8 (over z, core).
Axes of the slice: x: 2, y: 2, z: 4, core: 2. Of those that a mesh axis runs over, the one named last changes fastest.
Arguments:
- hidden: bfloat16 [36864, 5120], P(('grp', 'tp')), may hold values from -6 to 6
- lengths: int32 [4, 8], P('grp'), may hold values from 1 to 1152, 3686 in all within a row
- kv_weight: bfloat16 [5120, 1024], P('grp', 'tp'), may hold values from -0.078125 to 0.078125
- input_gain: float32 [5120], replicated, may hold values from 0.1 to 1.9
- key_gain: float32 [128], replicated, may hold values from 0.1 to 1.9
Outputs:
- cache_pages: bfloat16 [160, 128, 1024], P(('grp', 'tp'))
Inputs may be any that keep to these rules, and one draw needn't show every extreme that they name: In each group's row the 8 lengths sum to 3686 and the largest equals 1152.
All inputs are finite; a program needn't handle non-finite values.
Results may differ from a plain program's by a relative error of at most 0.0049.
Values may be sent and summed in bfloat16 or wider, within the bound.
No kernel may reach another device: no remote copies, remote signals or barrier semaphores. Data moves between devices by JAX's collectives and lax.ppermute only.
A program may use at most 64 MiB of HBM per device.

v0:
```python
import functools
import math

import jax
import jax.numpy as jnp
import numpy as np
from jax import lax
from jax.experimental import pallas as pl
from jax.experimental.pallas import tpu as pltpu
from jax.sharding import PartitionSpec as P

HD = 128
KVH = 4
BLK = 128


rope_base = 1000000.0
norm_eps = 1e-06


def normalize(token_rows, input_gain):
    values = token_rows.astype(jnp.float32)
    row_scale = lax.rsqrt(jnp.mean(values * values, axis=-1, keepdims=True) + norm_eps)
    return (values * row_scale * input_gain).astype(jnp.bfloat16)


def finish(projected, positions, valid, key_gain):
    key_width = KVH * HD
    half_dim = HD // 2
    row_count = projected.shape[0]
    key_part = projected[:, :key_width].reshape(row_count, KVH, HD)
    key_scale = lax.rsqrt(jnp.mean(key_part * key_part, axis=-1, keepdims=True) + norm_eps)
    key_part = key_part * key_scale * key_gain
    exponent = jnp.arange(half_dim, dtype=jnp.float32) * (2.0 / HD)
    inverse = jnp.exp(exponent * -math.log(rope_base))
    angles = positions.astype(jnp.float32)[:, None] * inverse[None, :]
    cosine = jnp.cos(angles)[:, None, :]
    sine_part = jnp.sin(angles)[:, None, :]
    lower_half = key_part[..., :half_dim]
    upper_half = key_part[..., half_dim:]
    turned = jnp.concatenate(
        [
            lower_half * cosine - upper_half * sine_part,
            upper_half * cosine + lower_half * sine_part,
        ],
        axis=-1,
    )
    merged = jnp.concatenate(
        [turned.reshape(row_count, key_width), projected[:, key_width:]], axis=-1
    )
    return jnp.where(valid[:, None], merged, 0.0).astype(jnp.bfloat16)


def project(normed, kv_weight):
    all_rows = lax.all_gather(kv_weight, "grp", axis=0, tiled=True)
    return jnp.dot(
        normed,
        lax.all_gather(all_rows, "tp", axis=1, tiled=True),
        preferred_element_type=jnp.float32,
    )


def group_tokens(tp_count, own_blocks):
    return 2 * tp_count * own_blocks * BLK // 5


def pages_per_device(tp_count, own_blocks):
    live_tokens = group_tokens(tp_count, own_blocks)
    return ((live_tokens + BLK - 1) // BLK + 2 * tp_count - 2) // tp_count


def general(hidden, lengths, kv_weight, input_gain, key_gain):
    tp_count = lax.axis_size("tp")
    my_index = lax.axis_index("tp")
    own_blocks = hidden.shape[0] // BLK
    page_count = pages_per_device(tp_count, own_blocks)
    per_peer = (own_blocks + tp_count - 1) // tp_count
    cache_width = 2 * KVH * HD
    group_len = lengths[0]
    block_counts = (group_len + (BLK - 1)) // BLK
    block_ends = jnp.cumsum(block_counts)
    block_starts = block_ends - block_counts
    offsets = jnp.arange(BLK, dtype=jnp.int32)
    my_start = block_starts[my_index]
    my_count = block_counts[my_index]
    my_length = group_len[my_index]
    outbound = (
        jnp.arange(tp_count, dtype=jnp.int32)[:, None] - my_start
    ) % tp_count + tp_count * jnp.arange(per_peer, dtype=jnp.int32)[None, :]
    outbound = outbound.reshape(-1)
    sending = outbound < my_count
    picked_local = jnp.minimum(outbound, own_blocks - 1)
    page_ranks = tp_count * jnp.arange(page_count, dtype=jnp.int32) + my_index
    anchor = jnp.minimum(
        jnp.sum((block_ends[None, :] <= page_ranks[:, None]).astype(jnp.int32), axis=1),
        tp_count - 1,
    )
    block_index = page_ranks - block_starts[anchor]
    page_live = page_ranks < block_ends[-1]
    chosen = anchor * per_peer + jnp.clip(block_index // tp_count, 0, per_peer - 1)
    projected = project(normalize(hidden, input_gain), kv_weight)
    own_pos = (jnp.arange(own_blocks, dtype=jnp.int32)[:, None] * BLK + offsets[None, :]).reshape(
        -1
    )
    own_cache = finish(projected, own_pos, own_pos < my_length, key_gain).reshape(
        own_blocks, BLK, cache_width
    )
    outgoing = jnp.where(
        sending[:, None, None],
        jnp.take(own_cache, picked_local, axis=0),
        jnp.zeros((), jnp.bfloat16),
    )
    arrived = lax.all_to_all(outgoing, "tp", split_axis=0, concat_axis=0, tiled=True)
    cache_pages = jnp.take(arrived, chosen, axis=0)
    return jnp.where(page_live[:, None, None], cache_pages, jnp.zeros((), jnp.bfloat16))


flip0 = [(i, i ^ 1) for i in range(4)]
flip1 = [(i, i ^ 2) for i in range(4)]


def sides(shard):
    return lax.ppermute(shard, "grp", flip0), lax.ppermute(shard, "grp", flip1)


def opposite(first_side0, second_side1):
    return lax.ppermute(first_side0, "grp", flip1), lax.ppermute(second_side1, "grp", flip0)


def stay(array):
    return pltpu.with_memory_space_constraint(array, pltpu.HBM)


def scale_kernel(lengths_ref, place_ref, x_ref, out_ref, x_buf, x_sem):
    count = (lengths_ref[place_ref[1]] + (BLK - 1)) // BLK

    def copy_of(block):
        rows = pl.ds(pl.multiple_of(block * BLK, BLK), BLK)
        return pltpu.make_async_copy(x_ref.at[rows], x_buf.at[rows], x_sem.at[block])

    def fetch(block, carry):
        copy_of(block).start()
        return carry

    def one_block(block, carry):
        copy_of(block).wait()
        rows = pl.ds(pl.multiple_of(block * BLK, BLK), BLK)
        squares = jnp.zeros((BLK, HD), jnp.float32)
        for cut in range(0, x_buf.shape[1], HD):
            values = x_buf[rows, cut : cut + HD].astype(jnp.float32)
            squares = squares + values * values
        mean = jnp.sum(squares, axis=-1, keepdims=True) / x_buf.shape[1]
        out_ref[rows, :] = jnp.broadcast_to(lax.rsqrt(mean + norm_eps), (BLK, HD))
        return carry

    lax.fori_loop(0, count, fetch, 0)
    lax.fori_loop(0, count, one_block, 0)


def row_scales(lengths, place, hidden):
    rows, width = hidden.shape
    small = pl.BlockSpec(memory_space=pltpu.SMEM)
    return pl.pallas_call(
        scale_kernel,
        in_specs=[small, small, pl.BlockSpec(memory_space=pltpu.HBM)],
        out_specs=pl.BlockSpec(memory_space=pltpu.VMEM),
        out_shape=jax.ShapeDtypeStruct((rows, HD), jnp.float32),
        scratch_shapes=[
            pltpu.VMEM((rows, width), hidden.dtype),
            pltpu.SemaphoreType.DMA((rows // BLK,)),
        ],
        compiler_params=pltpu.CompilerParams(vmem_limit_bytes=16 << 20),
        cost_estimate=pl.CostEstimate(
            flops=3 * rows * width, bytes_accessed=2 * rows * width, transcendentals=0
        ),
        name="row_scales",
    )(lengths, place, stay(hidden))


def tile_blocks(own_blocks):
    return max(t for t in (1, 2, 3) if own_blocks % t == 0)


class Chip:
    def __init__(self, lengths_ref, place_ref):
        self.tp_count = lengths_ref.shape[0]
        self.group, me = place_ref[0], place_ref[1]
        self.chip, self.core = me // 2, me % 2
        self.first = jnp.int32(0)
        for index in range(self.tp_count):
            count = (lengths_ref[index] + (BLK - 1)) // BLK
            self.first = self.first + jnp.where(index < 2 * self.chip, count, 0)
        length0, length1 = lengths_ref[2 * self.chip], lengths_ref[2 * self.chip + 1]
        self.count0 = (length0 + (BLK - 1)) // BLK
        self.own_len = jnp.where(self.core == 0, length0, length1)
        self.sib_len = jnp.where(self.core == 0, length1, length0)
        self.own_count = (self.own_len + (BLK - 1)) // BLK
        self.total = self.own_count + (self.sib_len + (BLK - 1)) // BLK

    def within(self, i):
        return jnp.where(i < self.own_count, i, i - self.own_count)

    def rows(self, i):
        return pl.ds(pl.multiple_of(self.within(i) * BLK, BLK), BLK)

    def fetch(self, i, own_ref, sib_ref, x_buf, x_sem, flips, depth, start):
        target = pl.ds(pl.multiple_of(i * BLK, BLK), BLK)

        def copies(source):
            for order, flip in enumerate(flips):
                columns = pl.ds(pl.multiple_of((self.group ^ flip) * depth, HD), depth)
                copy = pltpu.make_async_copy(
                    source.at[self.rows(i), columns],
                    x_buf.at[target, pl.ds(order * depth, depth)],
                    x_sem.at[i, order],
                )
                copy.start() if start else copy.wait()

        pl.when(i < self.own_count)(lambda: copies(own_ref))
        pl.when(jnp.logical_and(i >= self.own_count, i < self.total))(lambda: copies(sib_ref))

    def fetch_all(self, *args):
        def one_block(i, carry):
            self.fetch(i, *args, True)
            return carry

        lax.fori_loop(0, self.total, one_block, 0)


def near_kernel(tile, depth, pieces, *refs):
    lengths_ref, place_ref, own_ref, sib_ref = refs[:4]
    partial_ref, x_buf, w_buf, x_sem, w_sem = refs[-5:]
    near = refs[4:-5]
    chip = Chip(lengths_ref, place_ref)
    span = tile * BLK
    copies = [
        pltpu.make_async_copy(
            near[source].at[pl.ds(row, depth)],
            w_buf.at[pl.ds(part % 3 * depth, depth), pl.ds(part // 3 * HD, HD)],
            w_sem.at[part],
        )
        for part, (source, row) in enumerate(pieces)
    ]
    for copy in copies:
        copy.start()
    fetch = own_ref, sib_ref, x_buf, x_sem, (0, 1, 2), depth
    chip.fetch_all(*fetch)
    for copy in copies:
        copy.wait()

    def one_tile(step, carry):
        for part in range(tile):
            chip.fetch(step * tile + part, *fetch, False)
        rows = pl.ds(pl.multiple_of(step * span, span), span)
        partial_ref[rows, :] = jnp.dot(x_buf[rows, :], w_buf[...], preferred_element_type=jnp.float32)
        return carry

    lax.fori_loop(0, (chip.total + (tile - 1)) // tile, one_tile, 0)


def project_near(lengths, place, own, sibling, arrays, pieces, depth):
    rows, width = own.shape
    tile = tile_blocks(rows // BLK)
    columns = len(pieces) // 3 * HD
    small = pl.BlockSpec(memory_space=pltpu.SMEM)
    anywhere = pl.BlockSpec(memory_space=pl.ANY)
    in_hbm = pl.BlockSpec(memory_space=pltpu.HBM)
    held = 2 * rows + tile * BLK
    return pl.pallas_call(
        functools.partial(near_kernel, tile, depth, pieces),
        in_specs=[small] * 2 + [in_hbm] * 2 + [anywhere] * len(arrays),
        out_specs=pl.BlockSpec(memory_space=pltpu.VMEM),
        out_shape=jax.ShapeDtypeStruct((held, columns), jnp.float32),
        scratch_shapes=[
            pltpu.VMEM((held, 3 * depth), own.dtype),
            pltpu.VMEM((3 * depth, columns), jnp.bfloat16),
            pltpu.SemaphoreType.DMA((2 * rows // BLK, 3)),
            pltpu.SemaphoreType.DMA((len(pieces),)),
        ],
        compiler_params=pltpu.CompilerParams(vmem_limit_bytes=34 << 20),
        cost_estimate=pl.CostEstimate(
            flops=24 * rows * depth * columns, bytes_accessed=24 * rows * depth, transcendentals=0
        ),
        name="project_near",
    )(lengths, place, stay(own), stay(sibling), *arrays)


def far_kernel(slot_ids, tile, depth, deep, *refs):
    lengths_ref, place_ref, own_ref, sib_ref = refs[:4]
    far = refs[4:6]
    partial_ref, turn_ref, gain_ref, own_scale, sib_scale, out_ref, over_ref = refs[6:13]
    x_buf, w_buf, o_buf, x_sem, w_sem, o_sem = refs[13:]
    count = len(slot_ids)
    chip = Chip(lengths_ref, place_ref)
    tp_count, total, own_count = chip.tp_count, chip.total, chip.own_count
    tiles = (total + (tile - 1)) // tile
    span = tile * BLK
    copies = [
        pltpu.make_async_copy(far[index], w_buf.at[:, pl.ds(index * HD, HD)], w_sem.at[index])
        for index in range(count)
    ]
    for copy in copies:
        copy.start()
    fetch = own_ref, sib_ref, x_buf, x_sem, (3,), depth
    chip.fetch_all(*fetch)
    for copy in copies:
        copy.wait()
    is_key = [2 * (chip.chip ^ slot) + chip.core < KVH for slot in slot_ids]

    shift = tp_count.bit_length() - 1

    def send(i):
        second = jnp.where(i < own_count, chip.core, 1 - chip.core)
        place = chip.within(i) + second * chip.count0

        @pl.when(jnp.logical_and(i < total, place < deep * tp_count))
        def _():
            target = out_ref.at[(chip.first + place) & (tp_count - 1), lax.shift_right_logical(place, shift)]
            pltpu.make_async_copy(o_buf.at[i], target, o_sem.at[i]).start()

        @pl.when(jnp.logical_and(i < total, place >= deep * tp_count))
        def _():
            target = over_ref.at[place - deep * tp_count]
            pltpu.make_async_copy(o_buf.at[i], target, o_sem.at[i]).start()

    def multiply(step):
        for part in range(tile):
            chip.fetch(step * tile + part, *fetch, False)
        rows = pl.ds(pl.multiple_of(step * span, span), span)
        return partial_ref[rows, :] + jnp.dot(x_buf[rows, :], w_buf[...], preferred_element_type=jnp.float32)

    ones = jnp.full((HD, HD), 1.0 / HD, jnp.bfloat16)

    def head_mean(squares):
        high = squares.astype(jnp.bfloat16)
        low = (squares - high.astype(jnp.float32)).astype(jnp.bfloat16)
        return jnp.dot(high, ones, preferred_element_type=jnp.float32) + jnp.dot(
            low, ones, preferred_element_type=jnp.float32
        )

    def finish_tile(step, product):
        for part in range(tile):
            i = jnp.minimum(step * tile + part, total - 1)
            rows = chip.rows(i)
            limit = jnp.where(i < own_count, chip.own_len, chip.sib_len) - chip.within(i) * BLK
            valid = lax.broadcasted_iota(jnp.int32, (BLK, HD), 0) < limit
            scale = jnp.where(i < own_count, own_scale[rows, :], sib_scale[rows, :])
            for index in range(count):
                cut = product[part * BLK : (part + 1) * BLK, index * HD : (index + 1) * HD]
                values = cut * scale
                key_scale = lax.rsqrt(head_mean(values * values) + norm_eps)
                keys = values * key_scale * gain_ref[...]
                turned = keys * turn_ref[rows, :HD] + pltpu.roll(keys, HD // 2, 1) * turn_ref[rows, HD:]
                merged = jnp.where(jnp.logical_and(valid, is_key[index]), turned, jnp.where(valid, values, 0.0))
                o_buf[step * tile + part, index] = merged.astype(jnp.bfloat16)

    def send_tile(step):
        for part in range(tile):
            send(step * tile + part)

    def one_tile(step, product):
        following = multiply(step)
        finish_tile(step - 1, product)
        send_tile(step - 1)
        return following

    product = lax.fori_loop(1, tiles, one_tile, multiply(jnp.int32(0)))
    finish_tile(tiles - 1, product)
    send_tile(tiles - 1)

    def drain(i, carry):
        pltpu.make_async_copy(o_buf.at[i], out_ref.at[0, 0], o_sem.at[i]).wait()
        return carry

    lax.fori_loop(0, total, drain, 0)


def project_far(slot_ids, lengths, place, own, sibling, far, partial, scales, turn, key_gain, deep):
    rows, width = own.shape
    tp_count = lengths.shape[0]
    own_blocks = rows // BLK
    count = len(slot_ids)
    depth = far[0].shape[0]
    tile = tile_blocks(own_blocks)
    spare = 2 * own_blocks - deep * tp_count
    small = pl.BlockSpec(memory_space=pltpu.SMEM)
    anywhere = pl.BlockSpec(memory_space=pl.ANY)
    in_hbm = pl.BlockSpec(memory_space=pltpu.HBM)
    whole = pl.BlockSpec(memory_space=pltpu.VMEM)
    return pl.pallas_call(
        functools.partial(far_kernel, slot_ids, tile, depth, deep),
        in_specs=[small] * 2 + [in_hbm] * 2 + [anywhere] * 2 + [whole] * 5,
        out_specs=[in_hbm, anywhere],
        out_shape=[
            pltpu.HBM((tp_count, deep, count, BLK, HD), jnp.bfloat16),
            jax.ShapeDtypeStruct((max(spare, 1), count, BLK, HD), jnp.bfloat16),
        ],
        scratch_shapes=[
            pltpu.VMEM((2 * rows + tile * BLK, depth), own.dtype),
            pltpu.VMEM((depth, count * HD), jnp.bfloat16),
            pltpu.VMEM((2 * own_blocks + tile, count, BLK, HD), jnp.bfloat16),
            pltpu.SemaphoreType.DMA((2 * own_blocks, 1)),
            pltpu.SemaphoreType.DMA((count,)),
            pltpu.SemaphoreType.DMA((2 * own_blocks + tile,)),
        ],
        compiler_params=pltpu.CompilerParams(vmem_limit_bytes=16 << 20),
        cost_estimate=pl.CostEstimate(
            flops=16 * rows * depth * count * HD, bytes_accessed=16 * rows * depth, transcendentals=0
        ),
        name="project_far",
    )(lengths, place, stay(own), stay(sibling), *far, partial, turn, key_gain, *scales)


def page_source(lengths_ref, place_ref, page):
    tp_count = lengths_ref.shape[0]
    rank = page * tp_count + place_ref[1]
    end, chip, first = jnp.int32(0), jnp.int32(0), jnp.int32(0)
    for index in range(tp_count):
        end = end + (lengths_ref[index] + (BLK - 1)) // BLK
        if index % 2 == 1 and index + 1 < tp_count:
            passed = end <= rank
            chip = jnp.where(passed, index // 2 + 1, chip)
            first = jnp.where(passed, end, first)
    return rank < end, chip, rank - first


def columns_of(chip, slot, core):
    return pl.ds(pl.multiple_of((2 * (chip ^ slot) + core) * HD, HD), HD)


def early_kernel(groups, deep, lengths_ref, place_ref, *refs):
    arrived, spilled = refs[: len(groups)], refs[len(groups) : -3]
    out_ref, o_buf, o_sem = refs[-3:]
    tp_count = lengths_ref.shape[0]
    me = place_ref[1]

    def copy_of(page):
        return pltpu.make_async_copy(o_buf.at[page], out_ref.at[page], o_sem.at[page])

    for page in range(o_buf.shape[0]):
        live, chip, within = page_source(lengths_ref, place_ref, page)
        over = within >= deep * tp_count

        @pl.when(jnp.logical_and(live, jnp.logical_not(over)))
        def _():
            for order, slot_ids in enumerate(groups):
                for core in range(2):
                    for index, slot in enumerate(slot_ids):
                        block = arrived[order][2 * chip + core, within // tp_count, index]
                        o_buf[page, :, columns_of(chip, slot, core)] = block

        @pl.when(jnp.logical_and(live, over))
        def _():
            late = within - deep * tp_count
            for slot in range(tp_count // 2):
                o_buf[page, :, columns_of(chip, slot, me % 2)] = spilled[0][late, slot]
                o_buf[page, :, columns_of(chip, slot, 1 - me % 2)] = spilled[1][late, slot]

        @pl.when(jnp.logical_not(live))
        def _():
            o_buf[page] = jnp.zeros(o_buf.shape[1:], o_buf.dtype)

        copy_of(page).start()
    for page in range(o_buf.shape[0]):
        copy_of(page).wait()


def assemble_early(groups, lengths, place, arrived, spilled, page_count, deep):
    small = pl.BlockSpec(memory_space=pltpu.SMEM)
    whole = pl.BlockSpec(memory_space=pltpu.VMEM)
    shape = (page_count, BLK, 2 * KVH * HD)
    return pl.pallas_call(
        functools.partial(early_kernel, groups, deep),
        in_specs=[small] * 2 + [whole] * (len(arrived) + len(spilled)),
        out_specs=pl.BlockSpec(memory_space=pltpu.HBM),
        out_shape=pltpu.HBM(shape, jnp.bfloat16),
        scratch_shapes=[pltpu.VMEM(shape, jnp.bfloat16), pltpu.SemaphoreType.DMA((page_count,))],
        compiler_params=pltpu.CompilerParams(vmem_limit_bytes=16 << 20),
        name="assemble_early",
    )(lengths, place, *arrived, *spilled)


def late_kernel(slot_ids, deep, lengths_ref, place_ref, arrived, base_ref, out_ref, o_sem):
    del base_ref
    tp_count = lengths_ref.shape[0]

    def each_page(start):
        for page in range(out_ref.shape[0]):
            live, chip, within = page_source(lengths_ref, place_ref, page)

            @pl.when(jnp.logical_and(live, within < deep * tp_count))
            def _():
                for core in range(2):
                    for index, slot in enumerate(slot_ids):
                        copy = pltpu.make_async_copy(
                            arrived.at[2 * chip + core, within // tp_count, index],
                            out_ref.at[page, :, columns_of(chip, slot, core)],
                            o_sem.at[page, core, index],
                        )
                        copy.start() if start else copy.wait()

    each_page(True)
    each_page(False)


def assemble_late(slot_ids, lengths, place, arrived, base, deep):
    small = pl.BlockSpec(memory_space=pltpu.SMEM)
    return pl.pallas_call(
        functools.partial(late_kernel, slot_ids, deep),
        in_specs=[small] * 2 + [pl.BlockSpec(memory_space=pl.ANY), pl.BlockSpec(memory_space=pltpu.HBM)],
        out_specs=pl.BlockSpec(memory_space=pltpu.HBM),
        out_shape=pltpu.HBM(base.shape, base.dtype),
        scratch_shapes=[pltpu.SemaphoreType.DMA((base.shape[0], 2, len(slot_ids)))],
        input_output_aliases={3: 0},
        compiler_params=pltpu.CompilerParams(vmem_limit_bytes=16 << 20),
        name="assemble_late",
    )(lengths, place, arrived, base)


def rope_table(rows):
    inverse = np.exp(np.arange(HD // 2) * (-2.0 * math.log(rope_base) / HD))
    angles = np.arange(rows)[:, None] * inverse[None, :]
    cosine, sine_part = np.cos(angles), np.sin(angles)
    return jnp.asarray(np.concatenate([cosine, cosine, -sine_part, sine_part], axis=1), jnp.float32)


def exchange(sent):
    return lax.all_to_all(sent, "tp", split_axis=0, concat_axis=0, tiled=True)


def paired(hidden, lengths, kv_weight, input_gain, key_gain):
    tp_count = lax.axis_size("tp")
    nz = tp_count // 2
    group, me = lax.axis_index("grp"), lax.axis_index("tp")
    rows = hidden.shape[0]
    own_blocks = rows // BLK
    depth = kv_weight.shape[0]
    deep = 2 * own_blocks // tp_count
    page_count = pages_per_device(tp_count, own_blocks)
    group_len = lengths[0]
    place = jnp.stack([group, me]).astype(jnp.int32)
    swap = [(i, i ^ 1) for i in range(tp_count)]

    own_gain = lax.dynamic_slice(input_gain, (group * depth,), (depth,))
    shard = (kv_weight.astype(jnp.float32) * own_gain[:, None]).astype(jnp.bfloat16)
    sibling = lax.ppermute(hidden, "tp", swap)
    gain = key_gain.reshape(1, HD)

    def from_chip(flip, own):
        return lax.ppermute(own, "tp", [(i, i ^ (2 * flip)) for i in range(tp_count)])

    def start_group(arrays, pieces):
        return project_near(group_len, place, hidden, sibling, arrays, pieces, depth)

    def end_group(slot_ids, far, partial):
        return project_far(
            slot_ids, group_len, place, hidden, sibling, far, partial, (scale, other_scale), turn, gain, deep
        )

    groups = [tuple(range(start, min(start + 2, nz))) for start in range(0, nz, 2)]
    turn = rope_table(rows)
    slots = [shard] + [None] * (nz - 1)
    line = nz == 4
    inward = [(2 + c, 4 + c) for c in range(2)] + [(4 + c, 2 + c) for c in range(2)]
    outward = [(2 + c, c) for c in range(2)] + [(4 + c, 6 + c) for c in range(2)]
    slots[1] = from_chip(1, shard)
    side0 = sides(shard)
    across = lax.ppermute(shard, "tp", inward) if line else shard
    slots[1], shard, across = lax.optimization_barrier((slots[1], shard, across))
    if line:
        passed = lax.ppermute(slots[1], "tp", inward), lax.ppermute(across, "tp", outward)
    else:
        slots[2:] = [from_chip(flip, shard) for flip in range(2, nz)]
    slots[1], side0, later_len = lax.optimization_barrier((slots[1], side0, group_len))
    side1 = sides(slots[1])
    scale = row_scales(later_len, place, hidden)
    last = lax.ppermute(passed[0], "tp", outward) if line else None
    far = opposite(side0[0], side1[1])
    side1, scale, sibling = lax.optimization_barrier((side1, scale, sibling))
    other_scale = lax.ppermute(scale, "tp", swap)
    partial = start_group([slots[0], *side0, slots[1], *side1], [(part, 0) for part in range(6)])
    if line:
        far, other_scale, last, partial = lax.optimization_barrier((far, other_scale, last, partial))
        inner = (me // 2 == 1) | (me // 2 == 2)
        slots[2:] = [jnp.where(inner, passed[0], passed[1]), jnp.where(inner, across, last)]
    else:
        far, other_scale, slots, partial = lax.optimization_barrier((far, other_scale, slots, partial))
    sent, rest = end_group(groups[0], far, partial)
    arrived, over = [], [rest]
    for slot_ids in groups[1:]:
        both = jnp.concatenate([slots[slot] for slot in slot_ids])
        crossed = sides(both)
        arrived.append(exchange(sent))
        crossed, over[-1] = lax.optimization_barrier((crossed, over[-1]))
        far = opposite(crossed[0][:depth], crossed[1][depth:])
        pieces = [(source, index * depth) for index in range(2) for source in range(3)]
        partial = start_group([both, *crossed], pieces)
        far, partial = lax.optimization_barrier((far, partial))
        sent, rest = end_group(slot_ids, far, partial)
        over.append(rest)
    last_arrived = exchange(sent)

    def spill(rests):
        held = jnp.where(counts[me & -2] + counts[me | 1] > deep * tp_count, jnp.concatenate(rests, axis=1), 0)
        for flip in range(nz.bit_length() - 1):
            held = held + from_chip(1 << flip, held)
        return held, lax.ppermute(held, "tp", swap)

    def no_spill(rests):
        shape = (rests[0].shape[0], nz) + rests[0].shape[2:]
        return jnp.zeros(shape, jnp.bfloat16), jnp.zeros(shape, jnp.bfloat16)

    counts = (group_len + (BLK - 1)) // BLK
    most = jnp.max(counts[0::2] + counts[1::2])
    spilled = lax.cond(most > deep * tp_count, spill, no_spill, over)
    base = assemble_early(groups[:-1], group_len, place, arrived, spilled, page_count, deep)
    return assemble_late(groups[-1], group_len, place, last_arrived, base, deep)


def local(hidden, lengths, kv_weight, input_gain, key_gain):
    tp_count = lax.axis_size("tp")
    own_blocks = hidden.shape[0] // BLK
    spilling = (2 * own_blocks // tp_count * tp_count - 1) * BLK + 2
    fits = (
        lax.axis_size("grp") == 4
        and tp_count >= 4
        and tp_count & (tp_count - 1) == 0
        and kv_weight.shape[1] == HD
        and kv_weight.shape[0] % 256 == 0
        and 2 * own_blocks >= tp_count
        and 2 * spilling > group_tokens(tp_count, own_blocks)
    )
    chosen = paired if fits else general
    return chosen(hidden, lengths, kv_weight, input_gain, key_gain)


def solution(mesh):
    placed = (P(("grp", "tp"), None), P("grp", None), P("grp", "tp"), P(), P())
    return jax.shard_map(
        local, mesh=mesh, in_specs=placed, out_specs=P(("grp", "tp"), None, None), check_vma=False
    )
```

profile of v0, /device:TPU:0, one launch (start us, length us, event | category | flops | bytes accessed | tf_op | source)
XLA Modules:
  0.0 114.2 jit_solution(11616156665386331227)
XLA Ops:
  0.0 0.5 collective-permute-start.9
  0.5 0.8 dynamic_slice.9
  1.2 1.2 %multiply_convert_fusion.refs_4_ = bf16[1280,128]{1,0:T(8,128)(2,1)S(1)} fusion(bf16[1280,128]{1,0:T(8,128)(2,1)} %param.10, f32[1280]{0:T(1024)S(1)} %dynamic_slice.9), kind=kLoop, calls=%fused_computation.2 | loop fusion | flops 491520 | bytes 660480 | tf_op jit(solution)/shard_map/convert_element_type | solution.py:545
  2.4 2.6 %collective-permute-start.3 = (bf16[1280,128]{1,0:T(8,128)(2,1)S(1)}, bf16[1280,128]{1,0:T(8,128)(2,1)S(1)}, u32[]{:S(2)}, u32[]{:S(2)}) collective-permute-start(bf16[1280,128]{1,0:T(8,128)(2,1)S(1)} %multiply_convert_fusion.refs_4_), channel_id=1, source_target_pairs={{0,2},{1,3},{2,0},{3,1},{4,6},{5,7},{6,4},{7,5},{8,10},{9,11},{10,... | collective-permute-start | bytes 983048 | tf_op jit(solution)/shard_map/ppermute | solution.py:550
  5.1 0.7 collective-permute-start.4
  5.8 1.6 %collective-permute-start.5 = (bf16[1280,128]{1,0:T(8,128)(2,1)S(1)}, bf16[1280,128]{1,0:T(8,128)(2,1)}, u32[]{:S(2)}, u32[]{:S(2)}) collective-permute-start(bf16[1280,128]{1,0:T(8,128)(2,1)S(1)} %multiply_convert_fusion.refs_4_), channel_id=1, source_target_pairs={{0,8},{8,0},{16,24},{24,16},{1,9},{9,1},{17,25},{25,17},{2,10},{10... | collective-permute-start | bytes 983048 | tf_op jit(solution)/shard_map/ppermute | solution.py:123
  7.3 1.5 %collective-permute-start.6 = (bf16[1280,128]{1,0:T(8,128)(2,1)S(1)}, bf16[1280,128]{1,0:T(8,128)(2,1)S(1)}, u32[]{:S(2)}, u32[]{:S(2)}) collective-permute-start(bf16[1280,128]{1,0:T(8,128)(2,1)S(1)} %multiply_convert_fusion.refs_4_), channel_id=1, source_target_pairs={{0,16},{8,24},{16,0},{24,8},{1,17},{9,25},{17,1},{25,9},{2,18},{10... | collective-permute-start | bytes 983048 | tf_op jit(solution)/shard_map/ppermute | solution.py:123
  8.8 4.6 %collective-permute-done.3.refs_7_ = bf16[1280,128]{1,0:T(8,128)(2,1)S(1)} collective-permute-done((bf16[1280,128]{1,0:T(8,128)(2,1)S(1)}, bf16[1280,128]{1,0:T(8,128)(2,1)S(1)}, u32[]{:S(2)}, u32[]{:S(2)}) %collective-permute-start.3) | collective-permute-done | bytes 327712 | tf_op jit(solution)/shard_map/ppermute | solution.py:550
  13.5 2.3 %collective-permute-done.5.refs_5_ = bf16[1280,128]{1,0:T(8,128)(2,1)} collective-permute-done((bf16[1280,128]{1,0:T(8,128)(2,1)S(1)}, bf16[1280,128]{1,0:T(8,128)(2,1)}, u32[]{:S(2)}, u32[]{:S(2)}) %collective-permute-start.5) | collective-permute-done | bytes 327712 | tf_op jit(solution)/shard_map/ppermute | solution.py:123
  15.8 1.1 collective-permute-done.6.refs_6_
  16.9 1.5 %collective-permute-start.8 = (bf16[1280,128]{1,0:T(8,128)(2,1)S(1)}, bf16[1280,128]{1,0:T(8,128)(2,1)}, u32[]{:S(2)}, u32[]{:S(2)}) collective-permute-start(bf16[1280,128]{1,0:T(8,128)(2,1)S(1)} %collective-permute-done.3.refs_7_), channel_id=1, source_target_pairs={{0,16},{8,24},{16,0},{24,8},{1,17},{9,25},{17,1},{25,9},{2,18},{10... | collective-permute-start | bytes 983048 | tf_op jit(solution)/shard_map/ppermute | solution.py:123
  18.4 1.4 %collective-permute-start.10 = (bf16[1280,128]{1,0:T(8,128)(2,1)S(1)}, bf16[1280,128]{1,0:T(8,128)(2,1)}, u32[]{:S(2)}, u32[]{:S(2)}) collective-permute-start(bf16[1280,128]{1,0:T(8,128)(2,1)S(1)} %collective-permute-done.3.refs_7_), channel_id=1, source_target_pairs={{2,4},{3,5},{4,2},{5,3},{10,12},{11,13},{12,10},{13,11},{18,20},{1... | collective-permute-start | bytes 983048 | tf_op jit(solution)/shard_map/ppermute | solution.py:571
  19.8 1.3 %collective-permute-start.11 = (bf16[1280,128]{1,0:T(8,128)(2,1)S(1)}, bf16[1280,128]{1,0:T(8,128)(2,1)S(1)}, u32[]{:S(2)}, u32[]{:S(2)}) collective-permute-start(bf16[1280,128]{1,0:T(8,128)(2,1)S(1)} %collective-permute-done.4), channel_id=1, source_target_pairs={{2,0},{3,1},{4,6},{5,7},{10,8},{11,9},{12,14},{13,15},{18,16},{19,... | collective-permute-start | bytes 983048 | tf_op jit(solution)/shard_map/ppermute | solution.py:571
  21.2 0.6 collective-permute-start.7
  21.7 0.7 copy-done.1
  22.4 2.7 %row_scales.1.refs_9_ = f32[1152,128]{1,0:T(8,128)S(1)} custom-call(s32[8]{0:T(128)S(1)} %bitcast.6, s32[2]{0:T(128)S(1)} %pad_add_fusion.place_ref.refs_1_, bf16[1152,5120]{1,0:T(8,128)(2,1)} %refs_2_.7), custom_call_target="tpu_custom_call" | custom-call | flops 17694720 | bytes 11796480 | tf_op jit(solution)/shard_map/row_scales/pallas_call | solution.py:163
  25.1 0.6 collective-permute-done.8.refs_9_
  25.7 1.5 %collective-permute-start.12 = (bf16[1280,128]{1,0:T(8,128)(2,1)}, bf16[1280,128]{1,0:T(8,128)(2,1)S(1)}, u32[]{:S(2)}, u32[]{:S(2)}) collective-permute-start(bf16[1280,128]{1,0:T(8,128)(2,1)} %collective-permute-done.5.refs_5_), channel_id=1, source_target_pairs={{0,16},{8,24},{16,0},{24,8},{1,17},{9,25},{17,1},{25,9},{2,18},{10... | collective-permute-start | bytes 983048 | tf_op jit(solution)/shard_map/ppermute | solution.py:127
  27.2 2.6 %collective-permute-start.13 = (bf16[1280,128]{1,0:T(8,128)(2,1)}, bf16[1280,128]{1,0:T(8,128)(2,1)S(1)}, u32[]{:S(2)}, u32[]{:S(2)}) collective-permute-start(bf16[1280,128]{1,0:T(8,128)(2,1)} %collective-permute-done.8.refs_9_), channel_id=1, source_target_pairs={{0,8},{8,0},{16,24},{24,16},{1,9},{9,1},{17,25},{25,17},{2,10},{10... | collective-permute-start | bytes 983048 | tf_op jit(solution)/shard_map/ppermute | solution.py:127
  29.8 2.5 %collective-permute-done.11 = bf16[1280,128]{1,0:T(8,128)(2,1)S(1)} collective-permute-done((bf16[1280,128]{1,0:T(8,128)(2,1)S(1)}, bf16[1280,128]{1,0:T(8,128)(2,1)S(1)}, u32[]{:S(2)}, u32[]{:S(2)}) %collective-permute-start.11) | collective-permute-done | bytes 327712 | tf_op jit(solution)/shard_map/ppermute | solution.py:571
  32.4 1.3 %collective-permute-start.15 = (bf16[1280,128]{1,0:T(8,128)(2,1)}, bf16[1280,128]{1,0:T(8,128)(2,1)S(1)}, u32[]{:S(2)}, u32[]{:S(2)}) collective-permute-start(bf16[1280,128]{1,0:T(8,128)(2,1)} %collective-permute-done.10), channel_id=1, source_target_pairs={{2,0},{3,1},{4,6},{5,7},{10,8},{11,9},{12,14},{13,15},{18,16},{19,... | collective-permute-start | bytes 983048 | tf_op jit(solution)/shard_map/ppermute | solution.py:577
  33.8 5.1 %project_near.2.refs_6_ = f32[2688,256]{1,0:T(8,128)S(1)} custom-call(s32[8]{0:T(128)S(1)} %bitcast.7, s32[2]{0:T(128)S(1)} %pad_add_fusion.place_ref.refs_1_, bf16[1152,5120]{1,0:T(8,128)(2,1)} %refs_2_.7, bf16[1152,5120]{1,0:T(8,128)(2,1)} %collective-permute-done.9.refs_3_, bf16[1280,128]{1,0:T(8,128)(2,1)S(1)} %multiply_convert_fusion.refs_4_, ...), custom_call_target="tpu_custom_call" | custom-call | flops 9059696640 | bytes 35389440 | tf_op jit(solution)/shard_map/project_near/pallas_call | solution.py:269
  39.0 3.0 %collective-permute-done.15 = bf16[1280,128]{1,0:T(8,128)(2,1)S(1)} collective-permute-done((bf16[1280,128]{1,0:T(8,128)(2,1)}, bf16[1280,128]{1,0:T(8,128)(2,1)S(1)}, u32[]{:S(2)}, u32[]{:S(2)}) %collective-permute-start.15) | collective-permute-done | bytes 327712 | tf_op jit(solution)/shard_map/ppermute | solution.py:577
  42.0 0.9 pad_maximum_fusion.refs_4_
  42.9 0.9 collective-permute-start.16
  43.8 0.5 collective-permute-start.17
  44.3 4.5 %project_far.2 = (bf16[8,2,2,128,128]{4,3,2,1,0:T(8,128)(2,1)}, bf16[2,2,128,128]{3,2,1,0:T(8,128)(2,1)S(1)}) custom-call(s32[8]{0:T(128)S(1)} %bitcast.8, s32[2]{0:T(128)S(1)} %pad_add_fusion.place_ref.refs_1_, bf16[1152,5120]{1,0:T(8,128)(2,1)} %refs_2_.7, bf16[1152,5120]{1,0:T(8,128)(2,1)} %collective-permute-done.9.refs_3_, ...), custom_call_target="tpu_custom_call" | custom-call | flops 6039797760 | bytes 23592960 | tf_op jit(solution)/shard_map/project_far/pallas_call | solution.py:390
  48.8 7.2 %all-to-all-start.1 = ((bf16[8,2,2,128,128]{4,3,2,1,0:T(8,128)(2,1)}), bf16[8,2,2,128,128]{4,3,2,1,0:T(8,128)(2,1)S(1)}, u32[]{:S(2)}, u32[]{:S(2)}) async-start(bf16[8,2,2,128,128]{4,3,2,1,0:T(8,128)(2,1)} %get-tuple-element.66), calls=%async_computation.1 | async-start | bytes 2097152 | tf_op jit(solution)/shard_map/all_to_all | solution.py:528
  56.0 2.3 %collective-permute-done.16.refs_5_ = bf16[2560,128]{1,0:T(8,128)(2,1)} collective-permute-done((bf16[2560,128]{1,0:T(8,128)(2,1)}, bf16[2560,128]{1,0:T(8,128)(2,1)}, u32[]{:S(2)}, u32[]{:S(2)}) %collective-permute-start.16) | collective-permute-done | bytes 655392 | tf_op jit(solution)/shard_map/ppermute | solution.py:123
  58.3 1.5 %collective-permute-done.17.refs_6_ = bf16[2560,128]{1,0:T(8,128)(2,1)} collective-permute-done((bf16[2560,128]{1,0:T(8,128)(2,1)}, bf16[2560,128]{1,0:T(8,128)(2,1)}, u32[]{:S(2)}, u32[]{:S(2)}) %collective-permute-start.17) | collective-permute-done | bytes 655392 | tf_op jit(solution)/shard_map/ppermute | solution.py:123
  59.8 1.0 slice.12
  60.8 0.6 collective-permute-start.18
  61.4 1.0 slice.13
  62.3 0.4 collective-permute-start.19
  62.8 5.4 %project_near.3.refs_6_ = f32[2688,256]{1,0:T(8,128)S(1)} custom-call(s32[8]{0:T(128)S(1)} %bitcast.9, s32[2]{0:T(128)S(1)} %pad_add_fusion.place_ref.refs_1_, bf16[1152,5120]{1,0:T(8,128)(2,1)} %refs_2_.7, bf16[1152,5120]{1,0:T(8,128)(2,1)} %collective-permute-done.9.refs_3_, bf16[2560,128]{1,0:T(8,128)(2,1)} %pad_maximum_fusion.refs_4_, ...), custom_call_target="tpu_custom_call" | custom-call | flops 9059696640 | bytes 35389440 | tf_op jit(solution)/shard_map/project_near/pallas_call | solution.py:269
  68.1 0.4 collective-permute-done.18.refs_4_
  68.6 1.3 %collective-permute-done.19.refs_5_ = bf16[1280,128]{1,0:T(8,128)(2,1)S(1)} collective-permute-done((bf16[1280,128]{1,0:T(8,128)(2,1)S(1)}, bf16[1280,128]{1,0:T(8,128)(2,1)S(1)}, u32[]{:S(2)}, u32[]{:S(2)}) %collective-permute-start.19) | collective-permute-done | bytes 327712 | tf_op jit(solution)/shard_map/ppermute | solution.py:127
  69.9 4.4 %project_far.3 = (bf16[8,2,2,128,128]{4,3,2,1,0:T(8,128)(2,1)}, bf16[2,2,128,128]{3,2,1,0:T(8,128)(2,1)}) custom-call(s32[8]{0:T(128)S(1)} %bitcast.10, s32[2]{0:T(128)S(1)} %pad_add_fusion.place_ref.refs_1_, bf16[1152,5120]{1,0:T(8,128)(2,1)} %refs_2_.7, bf16[1152,5120]{1,0:T(8,128)(2,1)} %collective-permute-done.9.refs_3_, ...), custom_call_target="tpu_custom_call" | custom-call | flops 6039797760 | bytes 23592960 | tf_op jit(solution)/shard_map/project_far/pallas_call | solution.py:390
  74.3 8.3 %all-to-all-done.1.refs_0_ = bf16[8,2,2,128,128]{4,3,2,1,0:T(8,128)(2,1)S(1)} async-done(((bf16[8,2,2,128,128]{4,3,2,1,0:T(8,128)(2,1)}), bf16[8,2,2,128,128]{4,3,2,1,0:T(8,128)(2,1)S(1)}, u32[]{:S(2)}, u32[]{:S(2)}) %all-to-all-start.1) | async-done | bytes 1048608 | tf_op jit(solution)/shard_map/all_to_all | solution.py:528
  82.6 3.6 %all-to-all-start = ((bf16[8,2,2,128,128]{4,3,2,1,0:T(8,128)(2,1)}), bf16[8,2,2,128,128]{4,3,2,1,0:T(8,128)(2,1)S(1)}, u32[]{:S(2)}, u32[]{:S(2)}) async-start(bf16[8,2,2,128,128]{4,3,2,1,0:T(8,128)(2,1)} %get-tuple-element.65), calls=%async_computation | async-start | bytes 2097152 | tf_op jit(solution)/shard_map/all_to_all | solution.py:528
  86.2 0.1 slice.14
  86.4 0.6 add_reduce_fusion
  87.7 1.5 %conditional.1 = (bf16[2,4,128,128]{3,2,1,0:T(8,128)(2,1)}, bf16[2,4,128,128]{3,2,1,0:T(8,128)(2,1)}) conditional(s32[]{:T(128)} %convert_element_type.13, () %tuple.25, (s32[]{:T(128)}, s32[8]{0:T(128)S(1)}, bf16[2,2,128,128]{3,2,1,0:T(8,128)(2,1)S(1)}, bf16[2,2,128,128]{3,2,1,0:T(8,128)(2,1)S(1)}) %tuple.30), branch_computations={%region_1.2_spmd, %region_2.3_spmd} | conditional | flops 524298 | bytes 5243154 | solution.py:615
  87.7 0.7 broadcast.17
  88.4 0.7 broadcast.17.clone
  89.1 2.2 %assemble_early.1.base_ref = bf16[5,128,1024]{2,1,0:T(8,128)(2,1)} custom-call(s32[8]{0:T(128)S(1)} %bitcast.11, s32[2]{0:T(128)S(1)} %pad_add_fusion.place_ref.refs_1_, bf16[8,2,2,128,128]{4,3,2,1,0:T(8,128)(2,1)S(1)} %all-to-all-done.1.refs_0_, bf16[2,4,128,128]{3,2,1,0:T(8,128)(2,1)} %get-tuple-element.69.refs_1_, ...), custom_call_target="tpu_custom_call" | custom-call | tf_op jit(solution)/shard_map/assemble_early/pallas_call | solution.py:472
  91.4 21.3 %all-to-all-done.arrived = bf16[8,2,2,128,128]{4,3,2,1,0:T(8,128)(2,1)S(1)} async-done(((bf16[8,2,2,128,128]{4,3,2,1,0:T(8,128)(2,1)}), bf16[8,2,2,128,128]{4,3,2,1,0:T(8,128)(2,1)S(1)}, u32[]{:S(2)}, u32[]{:S(2)}) %all-to-all-start) | async-done | bytes 1048608 | tf_op jit(solution)/shard_map/all_to_all | solution.py:528
  112.7 1.5 %assemble_late.1 = bf16[5,128,1024]{2,1,0:T(8,128)(2,1)} custom-call(s32[8]{0:T(128)S(1)} %bitcast.12, s32[2]{0:T(128)S(1)} %pad_add_fusion.place_ref.refs_1_, bf16[8,2,2,128,128]{4,3,2,1,0:T(8,128)(2,1)S(1)} %all-to-all-done.arrived, bf16[5,128,1024]{2,1,0:T(8,128)(2,1)} %assemble_early.1.base_ref), custom_call_target="tpu_custom_call", output_to_operand_aliasing={{}: (3, {})} | custom-call | tf_op jit(solution)/shard_map/assemble_late/pallas_call | solution.py:508
  (26 shorter events, 0.4 us)
Async XLA Ops:
  0.0 33.7 %collective-permute-start.9 = (bf16[1152,5120]{1,0:T(8,128)(2,1)}, bf16[1152,5120]{1,0:T(8,128)(2,1)}, u32[]{:S(2)}, u32[]{:S(2)}) collective-permute-start(bf16[1152,5120]{1,0:T(8,128)(2,1)} %refs_2_.7), channel_id=1, source_target_pairs={{0,1},{1,0},{2,3},{3,2},{4,5},{5,4},{6,7},{7,6},{8,9},{9,8},{10,11... | collective-permute-start | bytes 35389448 | tf_op jit(solution)/shard_map/ppermute | solution.py:546
  2.4 11.0 %collective-permute-start.3 = (bf16[1280,128]{1,0:T(8,128)(2,1)S(1)}, bf16[1280,128]{1,0:T(8,128)(2,1)S(1)}, u32[]{:S(2)}, u32[]{:S(2)}) collective-permute-start(bf16[1280,128]{1,0:T(8,128)(2,1)S(1)} %multiply_convert_fusion.refs_4_), channel_id=1, source_target_pairs={{0,2},{1,3},{2,0},{3,1},{4,6},{5,7},{6,4},{7,5},{8,10},{9,11},{10,... | collective-permute-start | bytes 983048 | tf_op jit(solution)/shard_map/ppermute | solution.py:550
  5.1 8.4 %collective-permute-start.4 = (bf16[1280,128]{1,0:T(8,128)(2,1)S(1)}, bf16[1280,128]{1,0:T(8,128)(2,1)S(1)}, u32[]{:S(2)}, u32[]{:S(2)}) collective-permute-start(bf16[1280,128]{1,0:T(8,128)(2,1)S(1)} %multiply_convert_fusion.refs_4_), channel_id=1, source_target_pairs={{2,4},{3,5},{4,2},{5,3},{10,12},{11,13},{12,10},{13,11},{18,20},{1... | collective-permute-start | bytes 983048 | tf_op jit(solution)/shard_map/ppermute | solution.py:568
  5.8 10.0 %collective-permute-start.5 = (bf16[1280,128]{1,0:T(8,128)(2,1)S(1)}, bf16[1280,128]{1,0:T(8,128)(2,1)}, u32[]{:S(2)}, u32[]{:S(2)}) collective-permute-start(bf16[1280,128]{1,0:T(8,128)(2,1)S(1)} %multiply_convert_fusion.refs_4_), channel_id=1, source_target_pairs={{0,8},{8,0},{16,24},{24,16},{1,9},{9,1},{17,25},{25,17},{2,10},{10... | collective-permute-start | bytes 983048 | tf_op jit(solution)/shard_map/ppermute | solution.py:123
  7.3 9.6 %collective-permute-start.6 = (bf16[1280,128]{1,0:T(8,128)(2,1)S(1)}, bf16[1280,128]{1,0:T(8,128)(2,1)S(1)}, u32[]{:S(2)}, u32[]{:S(2)}) collective-permute-start(bf16[1280,128]{1,0:T(8,128)(2,1)S(1)} %multiply_convert_fusion.refs_4_), channel_id=1, source_target_pairs={{0,16},{8,24},{16,0},{24,8},{1,17},{9,25},{17,1},{25,9},{2,18},{10... | collective-permute-start | bytes 983048 | tf_op jit(solution)/shard_map/ppermute | solution.py:123
  13.5 11.6 %copy-start.4 = (bf16[1280,128]{1,0:T(8,128)(2,1)}, bf16[1280,128]{1,0:T(8,128)(2,1)S(1)}, u32[]{:S(2)}) copy-start(bf16[1280,128]{1,0:T(8,128)(2,1)S(1)} %collective-permute-done.4) | copy-start | bytes 983044
  16.9 8.8 %collective-permute-start.8 = (bf16[1280,128]{1,0:T(8,128)(2,1)S(1)}, bf16[1280,128]{1,0:T(8,128)(2,1)}, u32[]{:S(2)}, u32[]{:S(2)}) collective-permute-start(bf16[1280,128]{1,0:T(8,128)(2,1)S(1)} %collective-permute-done.3.refs_7_), channel_id=1, source_target_pairs={{0,16},{8,24},{16,0},{24,8},{1,17},{9,25},{17,1},{25,9},{2,18},{10... | collective-permute-start | bytes 983048 | tf_op jit(solution)/shard_map/ppermute | solution.py:123
  18.4 8.8 %collective-permute-start.10 = (bf16[1280,128]{1,0:T(8,128)(2,1)S(1)}, bf16[1280,128]{1,0:T(8,128)(2,1)}, u32[]{:S(2)}, u32[]{:S(2)}) collective-permute-start(bf16[1280,128]{1,0:T(8,128)(2,1)S(1)} %collective-permute-done.3.refs_7_), channel_id=1, source_target_pairs={{2,4},{3,5},{4,2},{5,3},{10,12},{11,13},{12,10},{13,11},{18,20},{1... | collective-permute-start | bytes 983048 | tf_op jit(solution)/shard_map/ppermute | solution.py:571
  19.8 12.6 %collective-permute-start.11 = (bf16[1280,128]{1,0:T(8,128)(2,1)S(1)}, bf16[1280,128]{1,0:T(8,128)(2,1)S(1)}, u32[]{:S(2)}, u32[]{:S(2)}) collective-permute-start(bf16[1280,128]{1,0:T(8,128)(2,1)S(1)} %collective-permute-done.4), channel_id=1, source_target_pairs={{2,0},{3,1},{4,6},{5,7},{10,8},{11,9},{12,14},{13,15},{18,16},{19,... | collective-permute-start | bytes 983048 | tf_op jit(solution)/shard_map/ppermute | solution.py:571
  21.2 12.6 %collective-permute-start.7 = (bf16[1280,128]{1,0:T(8,128)(2,1)S(1)}, bf16[1280,128]{1,0:T(8,128)(2,1)S(1)}, u32[]{:S(2)}, u32[]{:S(2)}) collective-permute-start(bf16[1280,128]{1,0:T(8,128)(2,1)S(1)} %collective-permute-done.3.refs_7_), channel_id=1, source_target_pairs={{0,8},{8,0},{16,24},{24,16},{1,9},{9,1},{17,25},{25,17},{2,10},{10... | collective-permute-start | bytes 983048 | tf_op jit(solution)/shard_map/ppermute | solution.py:123
  21.7 0.7 copy-start.1
  22.4 11.5 %copy-start.2 = (s32[1,8]{1,0:T(1,128)S(1)}, s32[1,8]{1,0:T(1,128)}, u32[]{:S(2)}) copy-start(s32[1,8]{1,0:T(1,128)} %param.9) | copy-start | bytes 100
  25.7 13.3 %collective-permute-start.12 = (bf16[1280,128]{1,0:T(8,128)(2,1)}, bf16[1280,128]{1,0:T(8,128)(2,1)S(1)}, u32[]{:S(2)}, u32[]{:S(2)}) collective-permute-start(bf16[1280,128]{1,0:T(8,128)(2,1)} %collective-permute-done.5.refs_5_), channel_id=1, source_target_pairs={{0,16},{8,24},{16,0},{24,8},{1,17},{9,25},{17,1},{25,9},{2,18},{10... | collective-permute-start | bytes 983048 | tf_op jit(solution)/shard_map/ppermute | solution.py:127
  27.2 11.8 %collective-permute-start.13 = (bf16[1280,128]{1,0:T(8,128)(2,1)}, bf16[1280,128]{1,0:T(8,128)(2,1)S(1)}, u32[]{:S(2)}, u32[]{:S(2)}) collective-permute-start(bf16[1280,128]{1,0:T(8,128)(2,1)} %collective-permute-done.8.refs_9_), channel_id=1, source_target_pairs={{0,8},{8,0},{16,24},{24,16},{1,9},{9,1},{17,25},{25,17},{2,10},{10... | collective-permute-start | bytes 983048 | tf_op jit(solution)/shard_map/ppermute | solution.py:127
  32.4 9.6 %collective-permute-start.15 = (bf16[1280,128]{1,0:T(8,128)(2,1)}, bf16[1280,128]{1,0:T(8,128)(2,1)S(1)}, u32[]{:S(2)}, u32[]{:S(2)}) collective-permute-start(bf16[1280,128]{1,0:T(8,128)(2,1)} %collective-permute-done.10), channel_id=1, source_target_pairs={{2,0},{3,1},{4,6},{5,7},{10,8},{11,9},{12,14},{13,15},{18,16},{19,... | collective-permute-start | bytes 983048 | tf_op jit(solution)/shard_map/ppermute | solution.py:577
  33.7 8.2 %copy-start.5 = (bf16[1280,128]{1,0:T(8,128)(2,1)S(1)}, bf16[1280,128]{1,0:T(8,128)(2,1)}, u32[]{:S(2)}) copy-start(bf16[1280,128]{1,0:T(8,128)(2,1)} %copy-done.4) | copy-start | bytes 983044
  33.8 8.2 %collective-permute-start.14 = (f32[1152,128]{1,0:T(8,128)S(1)}, f32[1152,128]{1,0:T(8,128)S(1)}, u32[]{:S(2)}, u32[]{:S(2)}) collective-permute-start(f32[1152,128]{1,0:T(8,128)S(1)} %row_scales.1.refs_9_), channel_id=1, source_target_pairs={{0,1},{1,0},{2,3},{3,2},{4,5},{5,4},{6,7},{7,6},{8,9},{9,8},{10,11... | collective-permute-start | bytes 1769480 | tf_op jit(solution)/shard_map/ppermute | solution.py:580
  39.0 5.3 %copy-start = (f32[1152,256]{1,0:T(8,128)S(1)}, f32[1152,256]{1,0:T(8,128)}, u32[]{:S(2)}) copy-start(f32[1152,256]{1,0:T(8,128)} %constant.66.clone.refs_7_) | copy-start | bytes 3538948
  39.0 5.3 %copy-start.3 = (f32[128]{0:T(128)S(1)}, f32[128]{0:T(128)}, u32[]{:S(2)}) copy-start(f32[128]{0:T(128)} %param.12) | copy-start | bytes 1540
  42.9 15.4 %collective-permute-start.16 = (bf16[2560,128]{1,0:T(8,128)(2,1)}, bf16[2560,128]{1,0:T(8,128)(2,1)}, u32[]{:S(2)}, u32[]{:S(2)}) collective-permute-start(bf16[2560,128]{1,0:T(8,128)(2,1)} %pad_maximum_fusion.refs_4_), channel_id=1, source_target_pairs={{0,8},{8,0},{16,24},{24,16},{1,9},{9,1},{17,25},{25,17},{2,10},{10... | collective-permute-start | bytes 1966088 | tf_op jit(solution)/shard_map/ppermute | solution.py:123
  43.8 16.0 %collective-permute-start.17 = (bf16[2560,128]{1,0:T(8,128)(2,1)}, bf16[2560,128]{1,0:T(8,128)(2,1)}, u32[]{:S(2)}, u32[]{:S(2)}) collective-permute-start(bf16[2560,128]{1,0:T(8,128)(2,1)} %pad_maximum_fusion.refs_4_), channel_id=1, source_target_pairs={{0,16},{8,24},{16,0},{24,8},{1,17},{9,25},{17,1},{25,9},{2,18},{10... | collective-permute-start | bytes 1966088 | tf_op jit(solution)/shard_map/ppermute | solution.py:123
  48.8 33.8 %all-to-all-start.1 = ((bf16[8,2,2,128,128]{4,3,2,1,0:T(8,128)(2,1)}), bf16[8,2,2,128,128]{4,3,2,1,0:T(8,128)(2,1)S(1)}, u32[]{:S(2)}, u32[]{:S(2)}) async-start(bf16[8,2,2,128,128]{4,3,2,1,0:T(8,128)(2,1)} %get-tuple-element.66), calls=%async_computation.1 | async-start | bytes 2097152 | tf_op jit(solution)/shard_map/all_to_all | solution.py:528
  60.8 7.8 %collective-permute-start.18 = (bf16[1280,128]{1,0:T(8,128)(2,1)S(1)}, bf16[1280,128]{1,0:T(8,128)(2,1)S(1)}, u32[]{:S(2)}, u32[]{:S(2)}) collective-permute-start(bf16[1280,128]{1,0:T(8,128)(2,1)S(1)} %slice.12), channel_id=1, source_target_pairs={{0,16},{8,24},{16,0},{24,8},{1,17},{9,25},{17,1},{25,9},{2,18},{10... | collective-permute-start | bytes 983048 | tf_op jit(solution)/shard_map/ppermute | solution.py:127
  62.3 7.5 %collective-permute-start.19 = (bf16[1280,128]{1,0:T(8,128)(2,1)S(1)}, bf16[1280,128]{1,0:T(8,128)(2,1)S(1)}, u32[]{:S(2)}, u32[]{:S(2)}) collective-permute-start(bf16[1280,128]{1,0:T(8,128)(2,1)S(1)} %slice.13), channel_id=1, source_target_pairs={{0,8},{8,0},{16,24},{24,16},{1,9},{9,1},{17,25},{25,17},{2,10},{10... | collective-permute-start | bytes 983048 | tf_op jit(solution)/shard_map/ppermute | solution.py:127
  74.3 13.4 %copy-start.6 = (bf16[2,2,128,128]{3,2,1,0:T(8,128)(2,1)S(1)}, bf16[2,2,128,128]{3,2,1,0:T(8,128)(2,1)}, u32[]{:S(2)}) copy-start(bf16[2,2,128,128]{3,2,1,0:T(8,128)(2,1)} %get-tuple-element.68) | copy-start | bytes 393220
  82.6 30.1 %all-to-all-start = ((bf16[8,2,2,128,128]{4,3,2,1,0:T(8,128)(2,1)}), bf16[8,2,2,128,128]{4,3,2,1,0:T(8,128)(2,1)S(1)}, u32[]{:S(2)}, u32[]{:S(2)}) async-start(bf16[8,2,2,128,128]{4,3,2,1,0:T(8,128)(2,1)} %get-tuple-element.65), calls=%async_computation | async-start | bytes 2097152 | tf_op jit(solution)/shard_map/all_to_all | solution.py:528
where the time goes:
time: 114 us
  waiting for transfers between devices  49.2 us (43%)
  starting transfers between devices  30.2 us (26%)
  Pallas kernels  25.8 us (23%)
  local copies, waits for them, and re-layouts  5.1 us (4%)
  other arithmetic  2.93 us (3%)
    all_to_all x2, waiting for transfers between devices, exchange(): return lax.all_to_all(sent, 'tp', split_axis=0, concat_axis=0, tiled=True)  29.6 us
    all_to_all x2, starting transfers between devices, exchange(): return lax.all_to_all(sent, 'tp', split_axis=0, concat_axis=0, tiled=True)  10.8 us
    pallas_call x2, Pallas kernels, project_near(): pl.pallas_call(functools.partial(near_kernel, tile, depth, pieces), in_sp...  10.5 us
    pallas_call x2, Pallas kernels, project_far(): pl.pallas_call(functools.partial(far_kernel, slot_ids, tile, depth, deep)...  8.85 us
    ppermute x1, waiting for transfers between devices, from_chip(): return lax.ppermute(own, 'tp', [(i, i ^ 2 * flip) for i in range(tp_count)])  4.64 us
    ppermute x3, waiting for transfers between devices, sides(): lax.ppermute(shard, 'grp', flip0)  4.61 us
    ppermute x3, starting transfers between devices, sides(): lax.ppermute(shard, 'grp', flip1)  3.55 us
    ppermute x3, waiting for transfers between devices, sides(): lax.ppermute(shard, 'grp', flip1)  3.18 us
  transfers between devices with their start and end apart: 19, of which 12 were waited for; matrix products, arithmetic and copies ran while one was open for 6% of the time, Pallas kernels for 21%

commit v1 on v0

--- a/solution.py
+++ b/solution.py
@@ -563,26 +563,27 @@
     line = nz == 4
     inward = [(2 + c, 4 + c) for c in range(2)] + [(4 + c, 2 + c) for c in range(2)]
     outward = [(2 + c, c) for c in range(2)] + [(4 + c, 6 + c) for c in range(2)]
+    around = inward + [(c, 6 + c) for c in range(2)] + [(6 + c, c) for c in range(2)]
+    inner = (me // 2 == 1) | (me // 2 == 2)
     slots[1] = from_chip(1, shard)
     side0 = sides(shard)
     across = lax.ppermute(shard, "tp", inward) if line else shard
     slots[1], shard, across = lax.optimization_barrier((slots[1], shard, across))
     if line:
-        passed = lax.ppermute(slots[1], "tp", inward), lax.ppermute(across, "tp", outward)
+        ends = lax.ppermute(jnp.where(inner, slots[1], shard), "tp", around)
+        passed = lax.ppermute(across, "tp", outward)
     else:
         slots[2:] = [from_chip(flip, shard) for flip in range(2, nz)]
     slots[1], side0, later_len = lax.optimization_barrier((slots[1], side0, group_len))
     side1 = sides(slots[1])
     scale = row_scales(later_len, place, hidden)
-    last = lax.ppermute(passed[0], "tp", outward) if line else None
     far = opposite(side0[0], side1[1])
     side1, scale, sibling = lax.optimization_barrier((side1, scale, sibling))
     other_scale = lax.ppermute(scale, "tp", swap)
     partial = start_group([slots[0], *side0, slots[1], *side1], [(part, 0) for part in range(6)])
     if line:
-        far, other_scale, last, partial = lax.optimization_barrier((far, other_scale, last, partial))
-        inner = (me // 2 == 1) | (me // 2 == 2)
-        slots[2:] = [jnp.where(inner, passed[0], passed[1]), jnp.where(inner, across, last)]
+        far, other_scale, ends, passed, partial = lax.optimization_barrier((far, other_scale, ends, passed, partial))
+        slots[2:] = [jnp.where(inner, ends, passed), jnp.where(inner, across, ends)]
     else:
         far, other_scale, slots, partial = lax.optimization_barrier((far, other_scale, slots, partial))
     sent, rest = end_group(groups[0], far, partial)

time: 114 us -> 112 us (0.982); the launches traced: 114 us -> 111 us
  waiting for transfers between devices: 49.2 us -> 47.2 us
    ppermute x3 -> x2, waiting for transfers between devices: 5.48 us -> 2.91 us  [the longest x1 2.91 us: paired(): passed = lax.ppermute(across, 'tp', outward)]
    ppermute x3, waiting for transfers between devices: 3.18 us -> 5.07 us  [sides(): lax.ppermute(shard, 'grp', flip1)]
    ppermute x2, starting transfers between devices: 2.09 us -> 0.89 us  [opposite(): lax.ppermute(first_side0, 'grp', flip1)]
    ppermute x3 -> x2, starting transfers between devices: 3.94 us -> 3.82 us  [the longest x1 2.54 us: paired(): ends = lax.ppermute(jnp.where(inner, slots[1], shard), 'tp', around)]
  transfers between devices with their start and end apart: 19 -> 18, of which waited for: 12 -> 10; matrix products, arithmetic and copies ran while one was open for 6% -> 6% of each run, Pallas kernels for 21% -> 22%
where the time goes in v1:
time: 112 us; the launch traced here: 111 us
  waiting for transfers between devices  47.2 us (42%)
  starting transfers between devices  29.4 us (26%)
  Pallas kernels  26.2 us (23%)
  local copies, waits for them, and re-layouts  4.47 us (4%)
  other arithmetic  2.95 us (3%)
    all_to_all x2, waiting for transfers between devices, exchange(): return lax.all_to_all(sent, 'tp', split_axis=0, concat_axis=0, tiled=True)  28.9 us
    all_to_all x2, starting transfers between devices, exchange(): return lax.all_to_all(sent, 'tp', split_axis=0, concat_axis=0, tiled=True)  10.7 us
    pallas_call x2, Pallas kernels, project_near(): pl.pallas_call(functools.partial(near_kernel, tile, depth, pieces), in_sp...  10.5 us
    pallas_call x2, Pallas kernels, project_far(): pl.pallas_call(functools.partial(far_kernel, slot_ids, tile, depth, deep)...  8.9 us
    ppermute x3, waiting for transfers between devices, sides(): lax.ppermute(shard, 'grp', flip0)  5.39 us
    ppermute x3, waiting for transfers between devices, sides(): lax.ppermute(shard, 'grp', flip1)  5.07 us
    ppermute x3, starting transfers between devices, sides(): lax.ppermute(shard, 'grp', flip1)  3.98 us
    ppermute x1, waiting for transfers between devices, from_chip(): return lax.ppermute(own, 'tp', [(i, i ^ 2 * flip) for i in range(tp_count)])  3.9 us
  transfers between devices with their start and end apart: 18, of which 10 were waited for; matrix products, arithmetic and copies ran while one was open for 6% of the time, Pallas kernels for 22%

profile of v1, /device:TPU:0, one launch (start us, length us, event | category | flops | bytes accessed | tf_op | source)
XLA Modules:
  0.0 111.1 jit_solution(1614649333895002660)
XLA Ops:
  0.0 0.5 collective-permute-start.9
  0.5 0.8 dynamic_slice.9
  1.2 1.2 %multiply_convert_fusion.refs_4_ = bf16[1280,128]{1,0:T(8,128)(2,1)S(1)} fusion(bf16[1280,128]{1,0:T(8,128)(2,1)} %param.10, f32[1280]{0:T(1024)S(1)} %dynamic_slice.9), kind=kLoop, calls=%fused_computation.2 | loop fusion | flops 491520 | bytes 660480 | tf_op jit(solution)/shard_map/convert_element_type | solution.py:545
  2.4 2.6 %collective-permute-start.3 = (bf16[1280,128]{1,0:T(8,128)(2,1)S(1)}, bf16[1280,128]{1,0:T(8,128)(2,1)S(1)}, u32[]{:S(2)}, u32[]{:S(2)}) collective-permute-start(bf16[1280,128]{1,0:T(8,128)(2,1)S(1)} %multiply_convert_fusion.refs_4_), channel_id=1, source_target_pairs={{0,2},{1,3},{2,0},{3,1},{4,6},{5,7},{6,4},{7,5},{8,10},{9,11},{10,... | collective-permute-start | bytes 983048 | tf_op jit(solution)/shard_map/ppermute | solution.py:550
  5.1 1.4 %collective-permute-start.4 = (bf16[1280,128]{1,0:T(8,128)(2,1)S(1)}, bf16[1280,128]{1,0:T(8,128)(2,1)}, u32[]{:S(2)}, u32[]{:S(2)}) collective-permute-start(bf16[1280,128]{1,0:T(8,128)(2,1)S(1)} %multiply_convert_fusion.refs_4_), channel_id=1, source_target_pairs={{2,4},{3,5},{4,2},{5,3},{10,12},{11,13},{12,10},{13,11},{18,20},{1... | collective-permute-start | bytes 983048 | tf_op jit(solution)/shard_map/ppermute | solution.py:570
  6.5 1.5 %collective-permute-start.5 = (bf16[1280,128]{1,0:T(8,128)(2,1)S(1)}, bf16[1280,128]{1,0:T(8,128)(2,1)S(1)}, u32[]{:S(2)}, u32[]{:S(2)}) collective-permute-start(bf16[1280,128]{1,0:T(8,128)(2,1)S(1)} %multiply_convert_fusion.refs_4_), channel_id=1, source_target_pairs={{0,8},{8,0},{16,24},{24,16},{1,9},{9,1},{17,25},{25,17},{2,10},{10... | collective-permute-start | bytes 983048 | tf_op jit(solution)/shard_map/ppermute | solution.py:123
  8.0 1.5 %collective-permute-start.6 = (bf16[1280,128]{1,0:T(8,128)(2,1)S(1)}, bf16[1280,128]{1,0:T(8,128)(2,1)S(1)}, u32[]{:S(2)}, u32[]{:S(2)}) collective-permute-start(bf16[1280,128]{1,0:T(8,128)(2,1)S(1)} %multiply_convert_fusion.refs_4_), channel_id=1, source_target_pairs={{0,16},{8,24},{16,0},{24,8},{1,17},{9,25},{17,1},{25,9},{2,18},{10... | collective-permute-start | bytes 983048 | tf_op jit(solution)/shard_map/ppermute | solution.py:123
  9.5 0.1 pad_add_fusion.place_ref.refs_1_
  9.6 3.9 %collective-permute-done.3.refs_7_ = bf16[1280,128]{1,0:T(8,128)(2,1)S(1)} collective-permute-done((bf16[1280,128]{1,0:T(8,128)(2,1)S(1)}, bf16[1280,128]{1,0:T(8,128)(2,1)S(1)}, u32[]{:S(2)}, u32[]{:S(2)}) %collective-permute-start.3) | collective-permute-done | bytes 327712 | tf_op jit(solution)/shard_map/ppermute | solution.py:550
  13.5 2.9 %collective-permute-done.5.refs_5_ = bf16[1280,128]{1,0:T(8,128)(2,1)S(1)} collective-permute-done((bf16[1280,128]{1,0:T(8,128)(2,1)S(1)}, bf16[1280,128]{1,0:T(8,128)(2,1)S(1)}, u32[]{:S(2)}, u32[]{:S(2)}) %collective-permute-start.5) | collective-permute-done | bytes 327712 | tf_op jit(solution)/shard_map/ppermute | solution.py:123
  16.3 1.2 %collective-permute-done.6.refs_6_ = bf16[1280,128]{1,0:T(8,128)(2,1)S(1)} collective-permute-done((bf16[1280,128]{1,0:T(8,128)(2,1)S(1)}, bf16[1280,128]{1,0:T(8,128)(2,1)S(1)}, u32[]{:S(2)}, u32[]{:S(2)}) %collective-permute-start.6) | collective-permute-done | bytes 327712 | tf_op jit(solution)/shard_map/ppermute | solution.py:123
  17.5 1.5 %collective-permute-start.8 = (bf16[1280,128]{1,0:T(8,128)(2,1)S(1)}, bf16[1280,128]{1,0:T(8,128)(2,1)S(1)}, u32[]{:S(2)}, u32[]{:S(2)}) collective-permute-start(bf16[1280,128]{1,0:T(8,128)(2,1)S(1)} %collective-permute-done.3.refs_7_), channel_id=1, source_target_pairs={{0,16},{8,24},{16,0},{24,8},{1,17},{9,25},{17,1},{25,9},{2,18},{10... | collective-permute-start | bytes 983048 | tf_op jit(solution)/shard_map/ppermute | solution.py:123
  19.0 0.5 collective-permute-start.7
  19.6 2.5 %collective-permute-start.13 = (bf16[1280,128]{1,0:T(8,128)(2,1)S(1)}, bf16[1280,128]{1,0:T(8,128)(2,1)S(1)}, u32[]{:S(2)}, u32[]{:S(2)}) collective-permute-start(bf16[1280,128]{1,0:T(8,128)(2,1)S(1)} %broadcast_select_fusion.2), channel_id=1, source_target_pairs={{2,4},{3,5},{4,2},{5,3},{0,6},{1,7},{6,0},{7,1},{10,12},{11,13},{1... | collective-permute-start | bytes 983048 | tf_op jit(solution)/shard_map/ppermute | solution.py:573
  22.2 0.5 collective-permute-start.10
  22.7 3.1 %row_scales.1.refs_9_ = f32[1152,128]{1,0:T(8,128)S(1)} custom-call(s32[8]{0:T(128)S(1)} %bitcast.6, s32[2]{0:T(128)S(1)} %pad_add_fusion.place_ref.refs_1_, bf16[1152,5120]{1,0:T(8,128)(2,1)} %refs_2_.7), custom_call_target="tpu_custom_call" | custom-call | flops 17694720 | bytes 11796480 | tf_op jit(solution)/shard_map/row_scales/pallas_call | solution.py:163
  25.8 2.4 %collective-permute-done.8.refs_9_ = bf16[1280,128]{1,0:T(8,128)(2,1)S(1)} collective-permute-done((bf16[1280,128]{1,0:T(8,128)(2,1)S(1)}, bf16[1280,128]{1,0:T(8,128)(2,1)S(1)}, u32[]{:S(2)}, u32[]{:S(2)}) %collective-permute-start.8) | collective-permute-done | bytes 327712 | tf_op jit(solution)/shard_map/ppermute | solution.py:123
  28.2 1.3 %collective-permute-start.14 = (bf16[1280,128]{1,0:T(8,128)(2,1)}, bf16[1280,128]{1,0:T(8,128)(2,1)S(1)}, u32[]{:S(2)}, u32[]{:S(2)}) collective-permute-start(bf16[1280,128]{1,0:T(8,128)(2,1)} %collective-permute-done.4), channel_id=1, source_target_pairs={{2,0},{3,1},{4,6},{5,7},{10,8},{11,9},{12,14},{13,15},{18,16},{19,... | collective-permute-start | bytes 983048 | tf_op jit(solution)/shard_map/ppermute | solution.py:574
  29.5 0.6 collective-permute-start.11
  30.1 5.1 %project_near.2.refs_6_ = f32[2688,256]{1,0:T(8,128)S(1)} custom-call(s32[8]{0:T(128)S(1)} %bitcast.7, s32[2]{0:T(128)S(1)} %pad_add_fusion.place_ref.refs_1_, bf16[1152,5120]{1,0:T(8,128)(2,1)} %refs_2_.7, bf16[1152,5120]{1,0:T(8,128)(2,1)} %collective-permute-done.9.refs_3_, bf16[1280,128]{1,0:T(8,128)(2,1)S(1)} %multiply_convert_fusion.refs_4_, ...), custom_call_target="tpu_custom_call" | custom-call | flops 9059696640 | bytes 35389440 | tf_op jit(solution)/shard_map/project_near/pallas_call | solution.py:269
  35.2 0.0 copy-start
  35.2 2.9 %collective-permute-done.14 = bf16[1280,128]{1,0:T(8,128)(2,1)S(1)} collective-permute-done((bf16[1280,128]{1,0:T(8,128)(2,1)}, bf16[1280,128]{1,0:T(8,128)(2,1)S(1)}, u32[]{:S(2)}, u32[]{:S(2)}) %collective-permute-start.14) | collective-permute-done | bytes 327712 | tf_op jit(solution)/shard_map/ppermute | solution.py:574
  38.2 0.1 broadcast_select_fusion.1
  38.2 0.9 pad_maximum_fusion.refs_4_
  39.2 1.1 collective-permute-start.15
  40.3 1.0 collective-permute-start.16
  41.2 4.5 %project_far.2 = (bf16[8,2,2,128,128]{4,3,2,1,0:T(8,128)(2,1)}, bf16[2,2,128,128]{3,2,1,0:T(8,128)(2,1)S(1)}) custom-call(s32[8]{0:T(128)S(1)} %bitcast.8, s32[2]{0:T(128)S(1)} %pad_add_fusion.place_ref.refs_1_, bf16[1152,5120]{1,0:T(8,128)(2,1)} %refs_2_.7, bf16[1152,5120]{1,0:T(8,128)(2,1)} %collective-permute-done.9.refs_3_, ...), custom_call_target="tpu_custom_call" | custom-call | flops 6039797760 | bytes 23592960 | tf_op jit(solution)/shard_map/project_far/pallas_call | solution.py:390
  45.7 7.2 %all-to-all-start.1 = ((bf16[8,2,2,128,128]{4,3,2,1,0:T(8,128)(2,1)}), bf16[8,2,2,128,128]{4,3,2,1,0:T(8,128)(2,1)S(1)}, u32[]{:S(2)}, u32[]{:S(2)}) async-start(bf16[8,2,2,128,128]{4,3,2,1,0:T(8,128)(2,1)} %get-tuple-element.70), calls=%async_computation.1 | async-start | bytes 2097152 | tf_op jit(solution)/shard_map/all_to_all | solution.py:528
  52.9 2.5 %collective-permute-done.15.refs_5_ = bf16[2560,128]{1,0:T(8,128)(2,1)} collective-permute-done((bf16[2560,128]{1,0:T(8,128)(2,1)}, bf16[2560,128]{1,0:T(8,128)(2,1)}, u32[]{:S(2)}, u32[]{:S(2)}) %collective-permute-start.15) | collective-permute-done | bytes 655392 | tf_op jit(solution)/shard_map/ppermute | solution.py:123
  55.4 1.5 %collective-permute-done.16.refs_6_ = bf16[2560,128]{1,0:T(8,128)(2,1)} collective-permute-done((bf16[2560,128]{1,0:T(8,128)(2,1)}, bf16[2560,128]{1,0:T(8,128)(2,1)}, u32[]{:S(2)}, u32[]{:S(2)}) %collective-permute-start.16) | collective-permute-done | bytes 655392 | tf_op jit(solution)/shard_map/ppermute | solution.py:123
  56.9 1.0 slice.12
  57.9 0.4 collective-permute-start.17
  58.2 1.0 slice.13
  59.2 1.8 %collective-permute-start.18 = (bf16[1280,128]{1,0:T(8,128)(2,1)S(1)}, bf16[1280,128]{1,0:T(8,128)(2,1)S(1)}, u32[]{:S(2)}, u32[]{:S(2)}) collective-permute-start(bf16[1280,128]{1,0:T(8,128)(2,1)S(1)} %slice.13), channel_id=1, source_target_pairs={{0,8},{8,0},{16,24},{24,16},{1,9},{9,1},{17,25},{25,17},{2,10},{10... | collective-permute-start | bytes 983048 | tf_op jit(solution)/shard_map/ppermute | solution.py:127
  61.0 5.3 %project_near.3.refs_6_ = f32[2688,256]{1,0:T(8,128)S(1)} custom-call(s32[8]{0:T(128)S(1)} %bitcast.9, s32[2]{0:T(128)S(1)} %pad_add_fusion.place_ref.refs_1_, bf16[1152,5120]{1,0:T(8,128)(2,1)} %refs_2_.7, bf16[1152,5120]{1,0:T(8,128)(2,1)} %collective-permute-done.9.refs_3_, bf16[2560,128]{1,0:T(8,128)(2,1)} %pad_maximum_fusion.refs_4_, ...), custom_call_target="tpu_custom_call" | custom-call | flops 9059696640 | bytes 35389440 | tf_op jit(solution)/shard_map/project_near/pallas_call | solution.py:269
  66.4 1.0 collective-permute-done.18.refs_5_
  67.4 4.4 %project_far.3 = (bf16[8,2,2,128,128]{4,3,2,1,0:T(8,128)(2,1)}, bf16[2,2,128,128]{3,2,1,0:T(8,128)(2,1)}) custom-call(s32[8]{0:T(128)S(1)} %bitcast.10, s32[2]{0:T(128)S(1)} %pad_add_fusion.place_ref.refs_1_, bf16[1152,5120]{1,0:T(8,128)(2,1)} %refs_2_.7, bf16[1152,5120]{1,0:T(8,128)(2,1)} %collective-permute-done.9.refs_3_, ...), custom_call_target="tpu_custom_call" | custom-call | flops 6039797760 | bytes 23592960 | tf_op jit(solution)/shard_map/project_far/pallas_call | solution.py:390
  71.8 7.6 %all-to-all-done.1.refs_0_ = bf16[8,2,2,128,128]{4,3,2,1,0:T(8,128)(2,1)S(1)} async-done(((bf16[8,2,2,128,128]{4,3,2,1,0:T(8,128)(2,1)}), bf16[8,2,2,128,128]{4,3,2,1,0:T(8,128)(2,1)S(1)}, u32[]{:S(2)}, u32[]{:S(2)}) %all-to-all-start.1) | async-done | bytes 1048608 | tf_op jit(solution)/shard_map/all_to_all | solution.py:528
  79.5 3.6 %all-to-all-start = ((bf16[8,2,2,128,128]{4,3,2,1,0:T(8,128)(2,1)}), bf16[8,2,2,128,128]{4,3,2,1,0:T(8,128)(2,1)S(1)}, u32[]{:S(2)}, u32[]{:S(2)}) async-start(bf16[8,2,2,128,128]{4,3,2,1,0:T(8,128)(2,1)} %get-tuple-element.69), calls=%async_computation | async-start | bytes 2097152 | tf_op jit(solution)/shard_map/all_to_all | solution.py:528
  83.0 0.1 slice.14
  83.1 0.1 slice.15
  83.2 0.6 add_reduce_fusion
  84.5 1.5 %conditional.1 = (bf16[2,4,128,128]{3,2,1,0:T(8,128)(2,1)}, bf16[2,4,128,128]{3,2,1,0:T(8,128)(2,1)}) conditional(s32[]{:T(128)} %convert_element_type.13, () %tuple.25, (s32[]{:T(128)}, s32[8]{0:T(128)S(1)}, bf16[2,2,128,128]{3,2,1,0:T(8,128)(2,1)S(1)}, bf16[2,2,128,128]{3,2,1,0:T(8,128)(2,1)S(1)}) %tuple.31), branch_computations={%region_1.2_spmd, %region_2.3_spmd} | conditional | flops 524298 | bytes 5243154 | solution.py:616
  84.5 0.7 broadcast.17
  85.3 0.8 broadcast.17.clone
  86.0 2.2 %assemble_early.1.base_ref = bf16[5,128,1024]{2,1,0:T(8,128)(2,1)} custom-call(s32[8]{0:T(128)S(1)} %bitcast.11, s32[2]{0:T(128)S(1)} %pad_add_fusion.place_ref.refs_1_, bf16[8,2,2,128,128]{4,3,2,1,0:T(8,128)(2,1)S(1)} %all-to-all-done.1.refs_0_, bf16[2,4,128,128]{3,2,1,0:T(8,128)(2,1)} %get-tuple-element.73.refs_1_, ...), custom_call_target="tpu_custom_call" | custom-call | tf_op jit(solution)/shard_map/assemble_early/pallas_call | solution.py:472
  88.3 21.3 %all-to-all-done.arrived = bf16[8,2,2,128,128]{4,3,2,1,0:T(8,128)(2,1)S(1)} async-done(((bf16[8,2,2,128,128]{4,3,2,1,0:T(8,128)(2,1)}), bf16[8,2,2,128,128]{4,3,2,1,0:T(8,128)(2,1)S(1)}, u32[]{:S(2)}, u32[]{:S(2)}) %all-to-all-start) | async-done | bytes 1048608 | tf_op jit(solution)/shard_map/all_to_all | solution.py:528
  109.5 1.5 %assemble_late.1 = bf16[5,128,1024]{2,1,0:T(8,128)(2,1)} custom-call(s32[8]{0:T(128)S(1)} %bitcast.12, s32[2]{0:T(128)S(1)} %pad_add_fusion.place_ref.refs_1_, bf16[8,2,2,128,128]{4,3,2,1,0:T(8,128)(2,1)S(1)} %all-to-all-done.arrived, bf16[5,128,1024]{2,1,0:T(8,128)(2,1)} %assemble_early.1.base_ref), custom_call_target="tpu_custom_call", output_to_operand_aliasing={{}: (3, {})} | custom-call | tf_op jit(solution)/shard_map/assemble_late/pallas_call | solution.py:508
  (18 shorter events, 0.1 us)
Async XLA Ops:
  0.0 22.7 %copy-start.1 = (s32[1,8]{1,0:T(1,128)S(1)}, s32[1,8]{1,0:T(1,128)}, u32[]{:S(2)}) copy-start(s32[1,8]{1,0:T(1,128)} %param.9) | copy-start | bytes 100
  0.0 30.1 %collective-permute-start.9 = (bf16[1152,5120]{1,0:T(8,128)(2,1)}, bf16[1152,5120]{1,0:T(8,128)(2,1)}, u32[]{:S(2)}, u32[]{:S(2)}) collective-permute-start(bf16[1152,5120]{1,0:T(8,128)(2,1)} %refs_2_.7), channel_id=1, source_target_pairs={{0,1},{1,0},{2,3},{3,2},{4,5},{5,4},{6,7},{7,6},{8,9},{9,8},{10,11... | collective-permute-start | bytes 35389448 | tf_op jit(solution)/shard_map/ppermute | solution.py:546
  2.4 11.0 %collective-permute-start.3 = (bf16[1280,128]{1,0:T(8,128)(2,1)S(1)}, bf16[1280,128]{1,0:T(8,128)(2,1)S(1)}, u32[]{:S(2)}, u32[]{:S(2)}) collective-permute-start(bf16[1280,128]{1,0:T(8,128)(2,1)S(1)} %multiply_convert_fusion.refs_4_), channel_id=1, source_target_pairs={{0,2},{1,3},{2,0},{3,1},{4,6},{5,7},{6,4},{7,5},{8,10},{9,11},{10,... | collective-permute-start | bytes 983048 | tf_op jit(solution)/shard_map/ppermute | solution.py:550
  5.1 8.4 %collective-permute-start.4 = (bf16[1280,128]{1,0:T(8,128)(2,1)S(1)}, bf16[1280,128]{1,0:T(8,128)(2,1)}, u32[]{:S(2)}, u32[]{:S(2)}) collective-permute-start(bf16[1280,128]{1,0:T(8,128)(2,1)S(1)} %multiply_convert_fusion.refs_4_), channel_id=1, source_target_pairs={{2,4},{3,5},{4,2},{5,3},{10,12},{11,13},{12,10},{13,11},{18,20},{1... | collective-permute-start | bytes 983048 | tf_op jit(solution)/shard_map/ppermute | solution.py:570
  6.5 9.8 %collective-permute-start.5 = (bf16[1280,128]{1,0:T(8,128)(2,1)S(1)}, bf16[1280,128]{1,0:T(8,128)(2,1)S(1)}, u32[]{:S(2)}, u32[]{:S(2)}) collective-permute-start(bf16[1280,128]{1,0:T(8,128)(2,1)S(1)} %multiply_convert_fusion.refs_4_), channel_id=1, source_target_pairs={{0,8},{8,0},{16,24},{24,16},{1,9},{9,1},{17,25},{25,17},{2,10},{10... | collective-permute-start | bytes 983048 | tf_op jit(solution)/shard_map/ppermute | solution.py:123
  8.0 9.6 %collective-permute-start.6 = (bf16[1280,128]{1,0:T(8,128)(2,1)S(1)}, bf16[1280,128]{1,0:T(8,128)(2,1)S(1)}, u32[]{:S(2)}, u32[]{:S(2)}) collective-permute-start(bf16[1280,128]{1,0:T(8,128)(2,1)S(1)} %multiply_convert_fusion.refs_4_), channel_id=1, source_target_pairs={{0,16},{8,24},{16,0},{24,8},{1,17},{9,25},{17,1},{25,9},{2,18},{10... | collective-permute-start | bytes 983048 | tf_op jit(solution)/shard_map/ppermute | solution.py:123
  17.5 10.6 %collective-permute-start.8 = (bf16[1280,128]{1,0:T(8,128)(2,1)S(1)}, bf16[1280,128]{1,0:T(8,128)(2,1)S(1)}, u32[]{:S(2)}, u32[]{:S(2)}) collective-permute-start(bf16[1280,128]{1,0:T(8,128)(2,1)S(1)} %collective-permute-done.3.refs_7_), channel_id=1, source_target_pairs={{0,16},{8,24},{16,0},{24,8},{1,17},{9,25},{17,1},{25,9},{2,18},{10... | collective-permute-start | bytes 983048 | tf_op jit(solution)/shard_map/ppermute | solution.py:123
  19.0 10.4 %collective-permute-start.7 = (bf16[1280,128]{1,0:T(8,128)(2,1)S(1)}, bf16[1280,128]{1,0:T(8,128)(2,1)S(1)}, u32[]{:S(2)}, u32[]{:S(2)}) collective-permute-start(bf16[1280,128]{1,0:T(8,128)(2,1)S(1)} %collective-permute-done.3.refs_7_), channel_id=1, source_target_pairs={{0,8},{8,0},{16,24},{24,16},{1,9},{9,1},{17,25},{25,17},{2,10},{10... | collective-permute-start | bytes 983048 | tf_op jit(solution)/shard_map/ppermute | solution.py:123
  19.6 15.6 %collective-permute-start.13 = (bf16[1280,128]{1,0:T(8,128)(2,1)S(1)}, bf16[1280,128]{1,0:T(8,128)(2,1)S(1)}, u32[]{:S(2)}, u32[]{:S(2)}) collective-permute-start(bf16[1280,128]{1,0:T(8,128)(2,1)S(1)} %broadcast_select_fusion.2), channel_id=1, source_target_pairs={{2,4},{3,5},{4,2},{5,3},{0,6},{1,7},{6,0},{7,1},{10,12},{11,13},{1... | collective-permute-start | bytes 983048 | tf_op jit(solution)/shard_map/ppermute | solution.py:573
  22.2 13.1 %collective-permute-start.10 = (bf16[1280,128]{1,0:T(8,128)(2,1)S(1)}, bf16[1280,128]{1,0:T(8,128)(2,1)S(1)}, u32[]{:S(2)}, u32[]{:S(2)}) collective-permute-start(bf16[1280,128]{1,0:T(8,128)(2,1)S(1)} %collective-permute-done.5.refs_5_), channel_id=1, source_target_pairs={{0,16},{8,24},{16,0},{24,8},{1,17},{9,25},{17,1},{25,9},{2,18},{10... | collective-permute-start | bytes 983048 | tf_op jit(solution)/shard_map/ppermute | solution.py:127
  28.2 10.0 %collective-permute-start.14 = (bf16[1280,128]{1,0:T(8,128)(2,1)}, bf16[1280,128]{1,0:T(8,128)(2,1)S(1)}, u32[]{:S(2)}, u32[]{:S(2)}) collective-permute-start(bf16[1280,128]{1,0:T(8,128)(2,1)} %collective-permute-done.4), channel_id=1, source_target_pairs={{2,0},{3,1},{4,6},{5,7},{10,8},{11,9},{12,14},{13,15},{18,16},{19,... | collective-permute-start | bytes 983048 | tf_op jit(solution)/shard_map/ppermute | solution.py:574
  29.5 8.7 %collective-permute-start.11 = (bf16[1280,128]{1,0:T(8,128)(2,1)S(1)}, bf16[1280,128]{1,0:T(8,128)(2,1)S(1)}, u32[]{:S(2)}, u32[]{:S(2)}) collective-permute-start(bf16[1280,128]{1,0:T(8,128)(2,1)S(1)} %collective-permute-done.8.refs_9_), channel_id=1, source_target_pairs={{0,8},{8,0},{16,24},{24,16},{1,9},{9,1},{17,25},{25,17},{2,10},{10... | collective-permute-start | bytes 983048 | tf_op jit(solution)/shard_map/ppermute | solution.py:127
  30.1 8.1 %collective-permute-start.12 = (f32[1152,128]{1,0:T(8,128)S(1)}, f32[1152,128]{1,0:T(8,128)S(1)}, u32[]{:S(2)}, u32[]{:S(2)}) collective-permute-start(f32[1152,128]{1,0:T(8,128)S(1)} %row_scales.1.refs_9_), channel_id=1, source_target_pairs={{0,1},{1,0},{2,3},{3,2},{4,5},{5,4},{6,7},{7,6},{8,9},{9,8},{10,11... | collective-permute-start | bytes 1769480 | tf_op jit(solution)/shard_map/ppermute | solution.py:582
  35.2 6.0 %copy-start = (f32[1152,256]{1,0:T(8,128)S(1)}, f32[1152,256]{1,0:T(8,128)}, u32[]{:S(2)}) copy-start(f32[1152,256]{1,0:T(8,128)} %constant.66.clone.refs_7_) | copy-start | bytes 3538948
  35.2 6.0 %copy-start.2 = (f32[128]{0:T(128)S(1)}, f32[128]{0:T(128)}, u32[]{:S(2)}) copy-start(f32[128]{0:T(128)} %param.12) | copy-start | bytes 1540
  39.2 16.2 %collective-permute-start.15 = (bf16[2560,128]{1,0:T(8,128)(2,1)}, bf16[2560,128]{1,0:T(8,128)(2,1)}, u32[]{:S(2)}, u32[]{:S(2)}) collective-permute-start(bf16[2560,128]{1,0:T(8,128)(2,1)} %pad_maximum_fusion.refs_4_), channel_id=1, source_target_pairs={{0,8},{8,0},{16,24},{24,16},{1,9},{9,1},{17,25},{25,17},{2,10},{10... | collective-permute-start | bytes 1966088 | tf_op jit(solution)/shard_map/ppermute | solution.py:123
  40.3 16.6 %collective-permute-start.16 = (bf16[2560,128]{1,0:T(8,128)(2,1)}, bf16[2560,128]{1,0:T(8,128)(2,1)}, u32[]{:S(2)}, u32[]{:S(2)}) collective-permute-start(bf16[2560,128]{1,0:T(8,128)(2,1)} %pad_maximum_fusion.refs_4_), channel_id=1, source_target_pairs={{0,16},{8,24},{16,0},{24,8},{1,17},{9,25},{17,1},{25,9},{2,18},{10... | collective-permute-start | bytes 1966088 | tf_op jit(solution)/shard_map/ppermute | solution.py:123
  45.7 33.8 %all-to-all-start.1 = ((bf16[8,2,2,128,128]{4,3,2,1,0:T(8,128)(2,1)}), bf16[8,2,2,128,128]{4,3,2,1,0:T(8,128)(2,1)S(1)}, u32[]{:S(2)}, u32[]{:S(2)}) async-start(bf16[8,2,2,128,128]{4,3,2,1,0:T(8,128)(2,1)} %get-tuple-element.70), calls=%async_computation.1 | async-start | bytes 2097152 | tf_op jit(solution)/shard_map/all_to_all | solution.py:528
  57.9 8.5 %collective-permute-start.17 = (bf16[1280,128]{1,0:T(8,128)(2,1)S(1)}, bf16[1280,128]{1,0:T(8,128)(2,1)S(1)}, u32[]{:S(2)}, u32[]{:S(2)}) collective-permute-start(bf16[1280,128]{1,0:T(8,128)(2,1)S(1)} %slice.12), channel_id=1, source_target_pairs={{0,16},{8,24},{16,0},{24,8},{1,17},{9,25},{17,1},{25,9},{2,18},{10... | collective-permute-start | bytes 983048 | tf_op jit(solution)/shard_map/ppermute | solution.py:127
  59.2 8.1 %collective-permute-start.18 = (bf16[1280,128]{1,0:T(8,128)(2,1)S(1)}, bf16[1280,128]{1,0:T(8,128)(2,1)S(1)}, u32[]{:S(2)}, u32[]{:S(2)}) collective-permute-start(bf16[1280,128]{1,0:T(8,128)(2,1)S(1)} %slice.13), channel_id=1, source_target_pairs={{0,8},{8,0},{16,24},{24,16},{1,9},{9,1},{17,25},{25,17},{2,10},{10... | collective-permute-start | bytes 983048 | tf_op jit(solution)/shard_map/ppermute | solution.py:127
  71.8 12.7 %copy-start.3 = (bf16[2,2,128,128]{3,2,1,0:T(8,128)(2,1)S(1)}, bf16[2,2,128,128]{3,2,1,0:T(8,128)(2,1)}, u32[]{:S(2)}) copy-start(bf16[2,2,128,128]{3,2,1,0:T(8,128)(2,1)} %get-tuple-element.72) | copy-start | bytes 393220
  79.5 30.1 %all-to-all-start = ((bf16[8,2,2,128,128]{4,3,2,1,0:T(8,128)(2,1)}), bf16[8,2,2,128,128]{4,3,2,1,0:T(8,128)(2,1)S(1)}, u32[]{:S(2)}, u32[]{:S(2)}) async-start(bf16[8,2,2,128,128]{4,3,2,1,0:T(8,128)(2,1)} %get-tuple-element.69), calls=%async_computation | async-start | bytes 2097152 | tf_op jit(solution)/shard_map/all_to_all | solution.py:528

commit v2 on v1

--- a/solution.py
+++ b/solution.py
@@ -601,18 +601,27 @@
         over.append(rest)
     last_arrived = exchange(sent)
 
+    counts = (group_len + (BLK - 1)) // BLK
+    chip_counts = counts[0::2] + counts[1::2]
+    most = jnp.max(chip_counts)
+
     def spill(rests):
-        held = jnp.where(counts[me & -2] + counts[me | 1] > deep * tp_count, jnp.concatenate(rests, axis=1), 0)
-        for flip in range(nz.bit_length() - 1):
-            held = held + from_chip(1 << flip, held)
-        return held, lax.ppermute(held, "tp", swap)
+        held = jnp.concatenate(rests, axis=1)
+        source = jnp.argmax(chip_counts).astype(jnp.int32)
+        first = jnp.sum(jnp.where(jnp.arange(nz) < source, chip_counts, 0))
+        moved = []
+        for late in range(held.shape[0]):
+            rank = deep * tp_count + late
+            flip = jnp.where(rank < most, source ^ ((first + rank) % tp_count // 2), 0)
+            ways = [lambda block: block] + [functools.partial(from_chip, way) for way in range(1, nz)]
+            moved.append(lax.switch(flip, ways, held[late]))
+        moved = jnp.stack(moved)
+        return moved, lax.ppermute(moved, "tp", swap)
 
     def no_spill(rests):
         shape = (rests[0].shape[0], nz) + rests[0].shape[2:]
         return jnp.zeros(shape, jnp.bfloat16), jnp.zeros(shape, jnp.bfloat16)
 
-    counts = (group_len + (BLK - 1)) // BLK
-    most = jnp.max(counts[0::2] + counts[1::2])
     spilled = lax.cond(most > deep * tp_count, spill, no_spill, over)
     base = assemble_early(groups[:-1], group_len, place, arrived, spilled, page_count, deep)
     return assemble_late(groups[-1], group_len, place, last_arrived, base, deep)

time: 112 us -> 111 us (level)
  Pallas kernels: 26.2 us -> 32.4 us
  waiting for transfers between devices: 47.2 us -> 41.1 us
    pallas_call x2, Pallas kernels: 10.5 us -> 14.3 us  [project_near(): pl.pallas_call(functools.partial(near_kernel, tile, depth, pieces), in_sp...]
    pallas_call x2, Pallas kernels: 8.9 us -> 11.7 us  [project_far(): pl.pallas_call(functools.partial(far_kernel, slot_ids, tile, depth, deep)...]
    all_to_all x2, waiting for transfers between devices: 28.9 us -> 26.5 us  [exchange(): return lax.all_to_all(sent, 'tp', split_axis=0, concat_axis=0, tiled=True)]
    ppermute x1, waiting for transfers between devices: 2.91 us -> 0.62 us  [paired(): passed = lax.ppermute(across, 'tp', outward)]
    all_to_all x2, starting transfers between devices: 10.7 us -> 9.04 us  [exchange(): return lax.all_to_all(sent, 'tp', split_axis=0, concat_axis=0, tiled=True)]
    ppermute x2, starting transfers between devices: 0.89 us -> 2.34 us  [opposite(): lax.ppermute(first_side0, 'grp', flip1)]
    ppermute x3, starting transfers between devices: 3.98 us -> 2.54 us  [sides(): lax.ppermute(shard, 'grp', flip1)]
  transfers between devices with their start and end apart: 18 -> 18, of which waited for: 10 -> 8; matrix products, arithmetic and copies ran while one was open for 6% -> 6% of each run, Pallas kernels for 22% -> 28%
where the time goes in v2:
time: 111 us
  waiting for transfers between devices  41.1 us (37%)
  Pallas kernels  32.4 us (29%)
  starting transfers between devices  29 us (26%)
  local copies, waits for them, and re-layouts  4.45 us (4%)
  other arithmetic  2.93 us (3%)
    all_to_all x2, waiting for transfers between devices, exchange(): return lax.all_to_all(sent, 'tp', split_axis=0, concat_axis=0, tiled=True)  26.5 us
    pallas_call x2, Pallas kernels, project_near(): pl.pallas_call(functools.partial(near_kernel, tile, depth, pieces), in_sp...  14.3 us
    pallas_call x2, Pallas kernels, project_far(): pl.pallas_call(functools.partial(far_kernel, slot_ids, tile, depth, deep)...  11.7 us
    all_to_all x2, starting transfers between devices, exchange(): return lax.all_to_all(sent, 'tp', split_axis=0, concat_axis=0, tiled=True)  9.04 us
    ppermute x3, waiting for transfers between devices, sides(): lax.ppermute(shard, 'grp', flip0)  5.29 us
    ppermute x3, waiting for transfers between devices, sides(): lax.ppermute(shard, 'grp', flip1)  4.69 us
    ppermute x3, starting transfers between devices, sides(): lax.ppermute(shard, 'grp', flip0)  3.91 us
    ppermute x1, waiting for transfers between devices, from_chip(): return lax.ppermute(own, 'tp', [(i, i ^ 2 * flip) for i in range(tp_count)])  3.91 us
  transfers between devices with their start and end apart: 18, of which 8 were waited for; matrix products, arithmetic and copies ran while one was open for 6% of the time, Pallas kernels for 28%

profile of v2, /device:TPU:0, one launch (start us, length us, event | category | flops | bytes accessed | tf_op | source)
XLA Modules:
  0.0 110.8 jit_solution(7833299130106407183)
XLA Ops:
  0.0 0.5 collective-permute-start.13
  0.5 0.8 dynamic_slice.3
  1.2 1.2 %multiply_convert_fusion.refs_4_ = bf16[1280,128]{1,0:T(8,128)(2,1)S(1)} fusion(bf16[1280,128]{1,0:T(8,128)(2,1)} %param.18, f32[1280]{0:T(1024)S(1)} %dynamic_slice.3), kind=kLoop, calls=%fused_computation.13 | loop fusion | flops 491520 | bytes 660480 | tf_op jit(solution)/shard_map/convert_element_type | solution.py:545
  2.4 2.6 %collective-permute-start.7 = (bf16[1280,128]{1,0:T(8,128)(2,1)S(1)}, bf16[1280,128]{1,0:T(8,128)(2,1)S(1)}, u32[]{:S(2)}, u32[]{:S(2)}) collective-permute-start(bf16[1280,128]{1,0:T(8,128)(2,1)S(1)} %multiply_convert_fusion.refs_4_), channel_id=1, source_target_pairs={{0,2},{1,3},{2,0},{3,1},{4,6},{5,7},{6,4},{7,5},{8,10},{9,11},{10,... | collective-permute-start | bytes 983048 | tf_op jit(solution)/shard_map/ppermute | solution.py:550
  5.1 1.4 %collective-permute-start.8 = (bf16[1280,128]{1,0:T(8,128)(2,1)S(1)}, bf16[1280,128]{1,0:T(8,128)(2,1)}, u32[]{:S(2)}, u32[]{:S(2)}) collective-permute-start(bf16[1280,128]{1,0:T(8,128)(2,1)S(1)} %multiply_convert_fusion.refs_4_), channel_id=1, source_target_pairs={{2,4},{3,5},{4,2},{5,3},{10,12},{11,13},{12,10},{13,11},{18,20},{1... | collective-permute-start | bytes 983048 | tf_op jit(solution)/shard_map/ppermute | solution.py:570
  6.5 1.5 %collective-permute-start.10 = (bf16[1280,128]{1,0:T(8,128)(2,1)S(1)}, bf16[1280,128]{1,0:T(8,128)(2,1)S(1)}, u32[]{:S(2)}, u32[]{:S(2)}) collective-permute-start(bf16[1280,128]{1,0:T(8,128)(2,1)S(1)} %multiply_convert_fusion.refs_4_), channel_id=1, source_target_pairs={{0,16},{8,24},{16,0},{24,8},{1,17},{9,25},{17,1},{25,9},{2,18},{10... | collective-permute-start | bytes 983048 | tf_op jit(solution)/shard_map/ppermute | solution.py:123
  8.0 1.5 %collective-permute-start.9 = (bf16[1280,128]{1,0:T(8,128)(2,1)S(1)}, bf16[1280,128]{1,0:T(8,128)(2,1)S(1)}, u32[]{:S(2)}, u32[]{:S(2)}) collective-permute-start(bf16[1280,128]{1,0:T(8,128)(2,1)S(1)} %multiply_convert_fusion.refs_4_), channel_id=1, source_target_pairs={{0,8},{8,0},{16,24},{24,16},{1,9},{9,1},{17,25},{25,17},{2,10},{10... | collective-permute-start | bytes 983048 | tf_op jit(solution)/shard_map/ppermute | solution.py:123
  9.5 0.1 pad_add_fusion.place_ref.refs_1_
  9.6 3.9 %collective-permute-done.7.refs_7_ = bf16[1280,128]{1,0:T(8,128)(2,1)S(1)} collective-permute-done((bf16[1280,128]{1,0:T(8,128)(2,1)S(1)}, bf16[1280,128]{1,0:T(8,128)(2,1)S(1)}, u32[]{:S(2)}, u32[]{:S(2)}) %collective-permute-start.7) | collective-permute-done | bytes 327712 | tf_op jit(solution)/shard_map/ppermute | solution.py:550
  13.5 0.0 collective-permute-done.8
  13.5 2.8 %collective-permute-done.10.refs_6_ = bf16[1280,128]{1,0:T(8,128)(2,1)S(1)} collective-permute-done((bf16[1280,128]{1,0:T(8,128)(2,1)S(1)}, bf16[1280,128]{1,0:T(8,128)(2,1)S(1)}, u32[]{:S(2)}, u32[]{:S(2)}) %collective-permute-start.10) | collective-permute-done | bytes 327712 | tf_op jit(solution)/shard_map/ppermute | solution.py:123
  16.3 1.2 %collective-permute-done.9.refs_5_ = bf16[1280,128]{1,0:T(8,128)(2,1)S(1)} collective-permute-done((bf16[1280,128]{1,0:T(8,128)(2,1)S(1)}, bf16[1280,128]{1,0:T(8,128)(2,1)S(1)}, u32[]{:S(2)}, u32[]{:S(2)}) %collective-permute-start.9) | collective-permute-done | bytes 327712 | tf_op jit(solution)/shard_map/ppermute | solution.py:123
  17.6 0.5 collective-permute-start.12
  18.1 1.5 %collective-permute-start.11 = (bf16[1280,128]{1,0:T(8,128)(2,1)S(1)}, bf16[1280,128]{1,0:T(8,128)(2,1)S(1)}, u32[]{:S(2)}, u32[]{:S(2)}) collective-permute-start(bf16[1280,128]{1,0:T(8,128)(2,1)S(1)} %collective-permute-done.7.refs_7_), channel_id=1, source_target_pairs={{0,8},{8,0},{16,24},{24,16},{1,9},{9,1},{17,25},{25,17},{2,10},{10... | collective-permute-start | bytes 983048 | tf_op jit(solution)/shard_map/ppermute | solution.py:123
  19.6 2.5 %collective-permute-start.17 = (bf16[1280,128]{1,0:T(8,128)(2,1)S(1)}, bf16[1280,128]{1,0:T(8,128)(2,1)S(1)}, u32[]{:S(2)}, u32[]{:S(2)}) collective-permute-start(bf16[1280,128]{1,0:T(8,128)(2,1)S(1)} %broadcast_select_fusion.2), channel_id=1, source_target_pairs={{2,4},{3,5},{4,2},{5,3},{0,6},{1,7},{6,0},{7,1},{10,12},{11,13},{1... | collective-permute-start | bytes 983048 | tf_op jit(solution)/shard_map/ppermute | solution.py:573
  22.1 1.5 %collective-permute-start.14 = (bf16[1280,128]{1,0:T(8,128)(2,1)S(1)}, bf16[1280,128]{1,0:T(8,128)(2,1)S(1)}, u32[]{:S(2)}, u32[]{:S(2)}) collective-permute-start(bf16[1280,128]{1,0:T(8,128)(2,1)S(1)} %collective-permute-done.9.refs_5_), channel_id=1, source_target_pairs={{0,16},{8,24},{16,0},{24,8},{1,17},{9,25},{17,1},{25,9},{2,18},{10... | collective-permute-start | bytes 983048 | tf_op jit(solution)/shard_map/ppermute | solution.py:127
  23.6 2.7 %row_scales.1.refs_9_ = f32[1152,128]{1,0:T(8,128)S(1)} custom-call(s32[8]{0:T(128)S(1)} %bitcast.23, s32[2]{0:T(128)S(1)} %pad_add_fusion.place_ref.refs_1_, bf16[1152,5120]{1,0:T(8,128)(2,1)} %refs_2_.7), custom_call_target="tpu_custom_call" | custom-call | flops 17694720 | bytes 11796480 | tf_op jit(solution)/shard_map/row_scales/pallas_call | solution.py:163
  26.4 1.8 %collective-permute-done.12.refs_9_ = bf16[1280,128]{1,0:T(8,128)(2,1)S(1)} collective-permute-done((bf16[1280,128]{1,0:T(8,128)(2,1)S(1)}, bf16[1280,128]{1,0:T(8,128)(2,1)S(1)}, u32[]{:S(2)}, u32[]{:S(2)}) %collective-permute-start.12) | collective-permute-done | bytes 327712 | tf_op jit(solution)/shard_map/ppermute | solution.py:123
  28.2 1.3 %collective-permute-start.18 = (bf16[1280,128]{1,0:T(8,128)(2,1)}, bf16[1280,128]{1,0:T(8,128)(2,1)S(1)}, u32[]{:S(2)}, u32[]{:S(2)}) collective-permute-start(bf16[1280,128]{1,0:T(8,128)(2,1)} %collective-permute-done.8), channel_id=1, source_target_pairs={{2,0},{3,1},{4,6},{5,7},{10,8},{11,9},{12,14},{13,15},{18,16},{19,... | collective-permute-start | bytes 983048 | tf_op jit(solution)/shard_map/ppermute | solution.py:574
  29.5 1.5 %collective-permute-start.15 = (bf16[1280,128]{1,0:T(8,128)(2,1)S(1)}, bf16[1280,128]{1,0:T(8,128)(2,1)S(1)}, u32[]{:S(2)}, u32[]{:S(2)}) collective-permute-start(bf16[1280,128]{1,0:T(8,128)(2,1)S(1)} %collective-permute-done.12.refs_9_), channel_id=1, source_target_pairs={{0,8},{8,0},{16,24},{24,16},{1,9},{9,1},{17,25},{25,17},{2,10},{10... | collective-permute-start | bytes 983048 | tf_op jit(solution)/shard_map/ppermute | solution.py:127
  31.1 7.0 %project_near.2.refs_6_ = f32[2688,256]{1,0:T(8,128)S(1)} custom-call(s32[8]{0:T(128)S(1)} %bitcast.24, s32[2]{0:T(128)S(1)} %pad_add_fusion.place_ref.refs_1_, bf16[1152,5120]{1,0:T(8,128)(2,1)} %refs_2_.7, bf16[1152,5120]{1,0:T(8,128)(2,1)} %collective-permute-done.13.refs_3_, bf16[1280,128]{1,0:T(8,128)(2,1)S(1)} %multiply_convert_fusion.refs_4_, ...), custom_call_target="tpu_custom_call" | custom-call | flops 9059696640 | bytes 35389440 | tf_op jit(solution)/shard_map/project_near/pallas_call | solution.py:269
  38.1 0.0 copy-start
  38.1 0.0 copy-start.2
  38.1 0.6 collective-permute-done.18
  38.7 0.1 broadcast_select_fusion.1
  38.8 0.9 pad_maximum_fusion.1.refs_4_
  39.7 0.9 collective-permute-start.19
  40.6 0.5 collective-permute-start.20
  41.2 5.9 %project_far.2 = (bf16[8,2,2,128,128]{4,3,2,1,0:T(8,128)(2,1)}, bf16[2,2,128,128]{3,2,1,0:T(8,128)(2,1)S(1)}) custom-call(s32[8]{0:T(128)S(1)} %bitcast.25, s32[2]{0:T(128)S(1)} %pad_add_fusion.place_ref.refs_1_, bf16[1152,5120]{1,0:T(8,128)(2,1)} %refs_2_.7, bf16[1152,5120]{1,0:T(8,128)(2,1)} %collective-permute-done.13.refs_3_, ...), custom_call_target="tpu_custom_call" | custom-call | flops 6039797760 | bytes 23592960 | tf_op jit(solution)/shard_map/project_far/pallas_call | solution.py:390
  47.1 5.5 %all-to-all-start.1 = ((bf16[8,2,2,128,128]{4,3,2,1,0:T(8,128)(2,1)}), bf16[8,2,2,128,128]{4,3,2,1,0:T(8,128)(2,1)S(1)}, u32[]{:S(2)}, u32[]{:S(2)}) async-start(bf16[8,2,2,128,128]{4,3,2,1,0:T(8,128)(2,1)} %get-tuple-element.109), calls=%async_computation.1 | async-start | bytes 2097152 | tf_op jit(solution)/shard_map/all_to_all | solution.py:528
  52.5 4.0 %collective-permute-done.19.refs_5_ = bf16[2560,128]{1,0:T(8,128)(2,1)} collective-permute-done((bf16[2560,128]{1,0:T(8,128)(2,1)}, bf16[2560,128]{1,0:T(8,128)(2,1)}, u32[]{:S(2)}, u32[]{:S(2)}) %collective-permute-start.19) | collective-permute-done | bytes 655392 | tf_op jit(solution)/shard_map/ppermute | solution.py:123
  56.6 1.0 slice.38
  57.6 0.8 collective-permute-start.21
  58.4 1.0 slice.39
  59.4 1.4 %collective-permute-start.22 = (bf16[1280,128]{1,0:T(8,128)(2,1)S(1)}, bf16[1280,128]{1,0:T(8,128)(2,1)S(1)}, u32[]{:S(2)}, u32[]{:S(2)}) collective-permute-start(bf16[1280,128]{1,0:T(8,128)(2,1)S(1)} %slice.39), channel_id=1, source_target_pairs={{0,8},{8,0},{16,24},{24,16},{1,9},{9,1},{17,25},{25,17},{2,10},{10... | collective-permute-start | bytes 983048 | tf_op jit(solution)/shard_map/ppermute | solution.py:127
  60.8 7.3 %project_near.3.refs_6_ = f32[2688,256]{1,0:T(8,128)S(1)} custom-call(s32[8]{0:T(128)S(1)} %bitcast.26, s32[2]{0:T(128)S(1)} %pad_add_fusion.place_ref.refs_1_, bf16[1152,5120]{1,0:T(8,128)(2,1)} %refs_2_.7, bf16[1152,5120]{1,0:T(8,128)(2,1)} %collective-permute-done.13.refs_3_, bf16[2560,128]{1,0:T(8,128)(2,1)} %pad_maximum_fusion.1.refs_4_, ...), custom_call_target="tpu_custom_call" | custom-call | flops 9059696640 | bytes 35389440 | tf_op jit(solution)/shard_map/project_near/pallas_call | solution.py:269
  68.1 5.8 %project_far.3 = (bf16[8,2,2,128,128]{4,3,2,1,0:T(8,128)(2,1)}, bf16[2,2,128,128]{3,2,1,0:T(8,128)(2,1)}) custom-call(s32[8]{0:T(128)S(1)} %bitcast.27, s32[2]{0:T(128)S(1)} %pad_add_fusion.place_ref.refs_1_, bf16[1152,5120]{1,0:T(8,128)(2,1)} %refs_2_.7, bf16[1152,5120]{1,0:T(8,128)(2,1)} %collective-permute-done.13.refs_3_, ...), custom_call_target="tpu_custom_call" | custom-call | flops 6039797760 | bytes 23592960 | tf_op jit(solution)/shard_map/project_far/pallas_call | solution.py:390
  73.9 5.3 %all-to-all-done.1.refs_0_ = bf16[8,2,2,128,128]{4,3,2,1,0:T(8,128)(2,1)S(1)} async-done(((bf16[8,2,2,128,128]{4,3,2,1,0:T(8,128)(2,1)}), bf16[8,2,2,128,128]{4,3,2,1,0:T(8,128)(2,1)S(1)}, u32[]{:S(2)}, u32[]{:S(2)}) %all-to-all-start.1) | async-done | bytes 1048608 | tf_op jit(solution)/shard_map/all_to_all | solution.py:528
  79.1 3.6 %all-to-all-start = ((bf16[8,2,2,128,128]{4,3,2,1,0:T(8,128)(2,1)}), bf16[8,2,2,128,128]{4,3,2,1,0:T(8,128)(2,1)S(1)}, u32[]{:S(2)}, u32[]{:S(2)}) async-start(bf16[8,2,2,128,128]{4,3,2,1,0:T(8,128)(2,1)} %get-tuple-element.108), calls=%async_computation | async-start | bytes 2097152 | tf_op jit(solution)/shard_map/all_to_all | solution.py:528
  82.7 0.1 slice.40
  82.8 0.1 slice.41
  82.9 0.6 fusion.1
  84.2 1.5 %conditional.3 = (bf16[2,4,128,128]{3,2,1,0:T(8,128)(2,1)}, bf16[2,4,128,128]{3,2,1,0:T(8,128)(2,1)}) conditional(s32[]{:T(128)} %convert_element_type.11, () %tuple.59, (s32[]{:T(128)}, s32[4]{0:T(128)S(1)}, bf16[2,2,128,128]{3,2,1,0:T(8,128)(2,1)S(1)}, bf16[2,2,128,128]{3,2,1,0:T(8,128)(2,1)S(1)}) %tuple.73), branch_computations={%region_1.2_spmd, %region_2.13_spmd} | conditional | flops 131166 | bytes 3670858 | solution.py:625
  84.2 0.7 broadcast.21
  85.0 0.7 broadcast.21.clone
  85.7 2.2 %assemble_early.1.base_ref = bf16[5,128,1024]{2,1,0:T(8,128)(2,1)} custom-call(s32[8]{0:T(128)S(1)} %bitcast.28, s32[2]{0:T(128)S(1)} %pad_add_fusion.place_ref.refs_1_, bf16[8,2,2,128,128]{4,3,2,1,0:T(8,128)(2,1)S(1)} %all-to-all-done.1.refs_0_, bf16[2,4,128,128]{3,2,1,0:T(8,128)(2,1)} %get-tuple-element.112.refs_1_, ...), custom_call_target="tpu_custom_call" | custom-call | tf_op jit(solution)/shard_map/assemble_early/pallas_call | solution.py:472
  87.9 21.3 %all-to-all-done.arrived = bf16[8,2,2,128,128]{4,3,2,1,0:T(8,128)(2,1)S(1)} async-done(((bf16[8,2,2,128,128]{4,3,2,1,0:T(8,128)(2,1)}), bf16[8,2,2,128,128]{4,3,2,1,0:T(8,128)(2,1)S(1)}, u32[]{:S(2)}, u32[]{:S(2)}) %all-to-all-start) | async-done | bytes 1048608 | tf_op jit(solution)/shard_map/all_to_all | solution.py:528
  109.2 1.5 %assemble_late.1 = bf16[5,128,1024]{2,1,0:T(8,128)(2,1)} custom-call(s32[8]{0:T(128)S(1)} %bitcast.29, s32[2]{0:T(128)S(1)} %pad_add_fusion.place_ref.refs_1_, bf16[8,2,2,128,128]{4,3,2,1,0:T(8,128)(2,1)S(1)} %all-to-all-done.arrived, bf16[5,128,1024]{2,1,0:T(8,128)(2,1)} %assemble_early.1.base_ref), custom_call_target="tpu_custom_call", output_to_operand_aliasing={{}: (3, {})} | custom-call | tf_op jit(solution)/shard_map/assemble_late/pallas_call | solution.py:508
  (18 shorter events, 0.1 us)
Async XLA Ops:
  0.0 23.6 %copy-start.1 = (s32[1,8]{1,0:T(1,128)S(1)}, s32[1,8]{1,0:T(1,128)}, u32[]{:S(2)}) copy-start(s32[1,8]{1,0:T(1,128)} %param.17) | copy-start | bytes 100
  0.0 31.0 %collective-permute-start.13 = (bf16[1152,5120]{1,0:T(8,128)(2,1)}, bf16[1152,5120]{1,0:T(8,128)(2,1)}, u32[]{:S(2)}, u32[]{:S(2)}) collective-permute-start(bf16[1152,5120]{1,0:T(8,128)(2,1)} %refs_2_.7), channel_id=1, source_target_pairs={{0,1},{1,0},{2,3},{3,2},{4,5},{5,4},{6,7},{7,6},{8,9},{9,8},{10,11... | collective-permute-start | bytes 35389448 | tf_op jit(solution)/shard_map/ppermute | solution.py:546
  2.4 11.0 %collective-permute-start.7 = (bf16[1280,128]{1,0:T(8,128)(2,1)S(1)}, bf16[1280,128]{1,0:T(8,128)(2,1)S(1)}, u32[]{:S(2)}, u32[]{:S(2)}) collective-permute-start(bf16[1280,128]{1,0:T(8,128)(2,1)S(1)} %multiply_convert_fusion.refs_4_), channel_id=1, source_target_pairs={{0,2},{1,3},{2,0},{3,1},{4,6},{5,7},{6,4},{7,5},{8,10},{9,11},{10,... | collective-permute-start | bytes 983048 | tf_op jit(solution)/shard_map/ppermute | solution.py:550
  5.1 8.4 %collective-permute-start.8 = (bf16[1280,128]{1,0:T(8,128)(2,1)S(1)}, bf16[1280,128]{1,0:T(8,128)(2,1)}, u32[]{:S(2)}, u32[]{:S(2)}) collective-permute-start(bf16[1280,128]{1,0:T(8,128)(2,1)S(1)} %multiply_convert_fusion.refs_4_), channel_id=1, source_target_pairs={{2,4},{3,5},{4,2},{5,3},{10,12},{11,13},{12,10},{13,11},{18,20},{1... | collective-permute-start | bytes 983048 | tf_op jit(solution)/shard_map/ppermute | solution.py:570
  6.5 9.8 %collective-permute-start.10 = (bf16[1280,128]{1,0:T(8,128)(2,1)S(1)}, bf16[1280,128]{1,0:T(8,128)(2,1)S(1)}, u32[]{:S(2)}, u32[]{:S(2)}) collective-permute-start(bf16[1280,128]{1,0:T(8,128)(2,1)S(1)} %multiply_convert_fusion.refs_4_), channel_id=1, source_target_pairs={{0,16},{8,24},{16,0},{24,8},{1,17},{9,25},{17,1},{25,9},{2,18},{10... | collective-permute-start | bytes 983048 | tf_op jit(solution)/shard_map/ppermute | solution.py:123
  8.0 9.6 %collective-permute-start.9 = (bf16[1280,128]{1,0:T(8,128)(2,1)S(1)}, bf16[1280,128]{1,0:T(8,128)(2,1)S(1)}, u32[]{:S(2)}, u32[]{:S(2)}) collective-permute-start(bf16[1280,128]{1,0:T(8,128)(2,1)S(1)} %multiply_convert_fusion.refs_4_), channel_id=1, source_target_pairs={{0,8},{8,0},{16,24},{24,16},{1,9},{9,1},{17,25},{25,17},{2,10},{10... | collective-permute-start | bytes 983048 | tf_op jit(solution)/shard_map/ppermute | solution.py:123
  17.6 10.6 %collective-permute-start.12 = (bf16[1280,128]{1,0:T(8,128)(2,1)S(1)}, bf16[1280,128]{1,0:T(8,128)(2,1)S(1)}, u32[]{:S(2)}, u32[]{:S(2)}) collective-permute-start(bf16[1280,128]{1,0:T(8,128)(2,1)S(1)} %collective-permute-done.7.refs_7_), channel_id=1, source_target_pairs={{0,16},{8,24},{16,0},{24,8},{1,17},{9,25},{17,1},{25,9},{2,18},{10... | collective-permute-start | bytes 983048 | tf_op jit(solution)/shard_map/ppermute | solution.py:123
  18.1 11.4 %collective-permute-start.11 = (bf16[1280,128]{1,0:T(8,128)(2,1)S(1)}, bf16[1280,128]{1,0:T(8,128)(2,1)S(1)}, u32[]{:S(2)}, u32[]{:S(2)}) collective-permute-start(bf16[1280,128]{1,0:T(8,128)(2,1)S(1)} %collective-permute-done.7.refs_7_), channel_id=1, source_target_pairs={{0,8},{8,0},{16,24},{24,16},{1,9},{9,1},{17,25},{25,17},{2,10},{10... | collective-permute-start | bytes 983048 | tf_op jit(solution)/shard_map/ppermute | solution.py:123
  19.6 18.5 %collective-permute-start.17 = (bf16[1280,128]{1,0:T(8,128)(2,1)S(1)}, bf16[1280,128]{1,0:T(8,128)(2,1)S(1)}, u32[]{:S(2)}, u32[]{:S(2)}) collective-permute-start(bf16[1280,128]{1,0:T(8,128)(2,1)S(1)} %broadcast_select_fusion.2), channel_id=1, source_target_pairs={{2,4},{3,5},{4,2},{5,3},{0,6},{1,7},{6,0},{7,1},{10,12},{11,13},{1... | collective-permute-start | bytes 983048 | tf_op jit(solution)/shard_map/ppermute | solution.py:573
  22.1 16.0 %collective-permute-start.14 = (bf16[1280,128]{1,0:T(8,128)(2,1)S(1)}, bf16[1280,128]{1,0:T(8,128)(2,1)S(1)}, u32[]{:S(2)}, u32[]{:S(2)}) collective-permute-start(bf16[1280,128]{1,0:T(8,128)(2,1)S(1)} %collective-permute-done.9.refs_5_), channel_id=1, source_target_pairs={{0,16},{8,24},{16,0},{24,8},{1,17},{9,25},{17,1},{25,9},{2,18},{10... | collective-permute-start | bytes 983048 | tf_op jit(solution)/shard_map/ppermute | solution.py:127
  28.2 10.5 %collective-permute-start.18 = (bf16[1280,128]{1,0:T(8,128)(2,1)}, bf16[1280,128]{1,0:T(8,128)(2,1)S(1)}, u32[]{:S(2)}, u32[]{:S(2)}) collective-permute-start(bf16[1280,128]{1,0:T(8,128)(2,1)} %collective-permute-done.8), channel_id=1, source_target_pairs={{2,0},{3,1},{4,6},{5,7},{10,8},{11,9},{12,14},{13,15},{18,16},{19,... | collective-permute-start | bytes 983048 | tf_op jit(solution)/shard_map/ppermute | solution.py:574
  29.5 9.2 %collective-permute-start.15 = (bf16[1280,128]{1,0:T(8,128)(2,1)S(1)}, bf16[1280,128]{1,0:T(8,128)(2,1)S(1)}, u32[]{:S(2)}, u32[]{:S(2)}) collective-permute-start(bf16[1280,128]{1,0:T(8,128)(2,1)S(1)} %collective-permute-done.12.refs_9_), channel_id=1, source_target_pairs={{0,8},{8,0},{16,24},{24,16},{1,9},{9,1},{17,25},{25,17},{2,10},{10... | collective-permute-start | bytes 983048 | tf_op jit(solution)/shard_map/ppermute | solution.py:127
  31.0 7.7 %collective-permute-start.16 = (f32[1152,128]{1,0:T(8,128)S(1)}, f32[1152,128]{1,0:T(8,128)S(1)}, u32[]{:S(2)}, u32[]{:S(2)}) collective-permute-start(f32[1152,128]{1,0:T(8,128)S(1)} %row_scales.1.refs_9_), channel_id=1, source_target_pairs={{0,1},{1,0},{2,3},{3,2},{4,5},{5,4},{6,7},{7,6},{8,9},{9,8},{10,11... | collective-permute-start | bytes 1769480 | tf_op jit(solution)/shard_map/ppermute | solution.py:582
  38.1 3.1 %copy-start = (f32[1152,256]{1,0:T(8,128)S(1)}, f32[1152,256]{1,0:T(8,128)}, u32[]{:S(2)}) copy-start(f32[1152,256]{1,0:T(8,128)} %constant.100.clone.refs_7_) | copy-start | bytes 3538948
  38.1 3.1 %copy-start.2 = (f32[128]{0:T(128)S(1)}, f32[128]{0:T(128)}, u32[]{:S(2)}) copy-start(f32[128]{0:T(128)} %param.20) | copy-start | bytes 1540
  39.7 16.9 %collective-permute-start.19 = (bf16[2560,128]{1,0:T(8,128)(2,1)}, bf16[2560,128]{1,0:T(8,128)(2,1)}, u32[]{:S(2)}, u32[]{:S(2)}) collective-permute-start(bf16[2560,128]{1,0:T(8,128)(2,1)} %pad_maximum_fusion.1.refs_4_), channel_id=1, source_target_pairs={{0,8},{8,0},{16,24},{24,16},{1,9},{9,1},{17,25},{25,17},{2,10},{10... | collective-permute-start | bytes 1966088 | tf_op jit(solution)/shard_map/ppermute | solution.py:123
  40.6 15.9 %collective-permute-start.20 = (bf16[2560,128]{1,0:T(8,128)(2,1)}, bf16[2560,128]{1,0:T(8,128)(2,1)}, u32[]{:S(2)}, u32[]{:S(2)}) collective-permute-start(bf16[2560,128]{1,0:T(8,128)(2,1)} %pad_maximum_fusion.1.refs_4_), channel_id=1, source_target_pairs={{0,16},{8,24},{16,0},{24,8},{1,17},{9,25},{17,1},{25,9},{2,18},{10... | collective-permute-start | bytes 1966088 | tf_op jit(solution)/shard_map/ppermute | solution.py:123
  47.1 32.1 %all-to-all-start.1 = ((bf16[8,2,2,128,128]{4,3,2,1,0:T(8,128)(2,1)}), bf16[8,2,2,128,128]{4,3,2,1,0:T(8,128)(2,1)S(1)}, u32[]{:S(2)}, u32[]{:S(2)}) async-start(bf16[8,2,2,128,128]{4,3,2,1,0:T(8,128)(2,1)} %get-tuple-element.109), calls=%async_computation.1 | async-start | bytes 2097152 | tf_op jit(solution)/shard_map/all_to_all | solution.py:528
  57.6 10.5 %collective-permute-start.21 = (bf16[1280,128]{1,0:T(8,128)(2,1)S(1)}, bf16[1280,128]{1,0:T(8,128)(2,1)S(1)}, u32[]{:S(2)}, u32[]{:S(2)}) collective-permute-start(bf16[1280,128]{1,0:T(8,128)(2,1)S(1)} %slice.38), channel_id=1, source_target_pairs={{0,16},{8,24},{16,0},{24,8},{1,17},{9,25},{17,1},{25,9},{2,18},{10... | collective-permute-start | bytes 983048 | tf_op jit(solution)/shard_map/ppermute | solution.py:127
  59.4 8.6 %collective-permute-start.22 = (bf16[1280,128]{1,0:T(8,128)(2,1)S(1)}, bf16[1280,128]{1,0:T(8,128)(2,1)S(1)}, u32[]{:S(2)}, u32[]{:S(2)}) collective-permute-start(bf16[1280,128]{1,0:T(8,128)(2,1)S(1)} %slice.39), channel_id=1, source_target_pairs={{0,8},{8,0},{16,24},{24,16},{1,9},{9,1},{17,25},{25,17},{2,10},{10... | collective-permute-start | bytes 983048 | tf_op jit(solution)/shard_map/ppermute | solution.py:127
  73.9 10.3 %copy-start.3 = (bf16[2,2,128,128]{3,2,1,0:T(8,128)(2,1)S(1)}, bf16[2,2,128,128]{3,2,1,0:T(8,128)(2,1)}, u32[]{:S(2)}) copy-start(bf16[2,2,128,128]{3,2,1,0:T(8,128)(2,1)} %get-tuple-element.111) | copy-start | bytes 393220
  79.1 30.1 %all-to-all-start = ((bf16[8,2,2,128,128]{4,3,2,1,0:T(8,128)(2,1)}), bf16[8,2,2,128,128]{4,3,2,1,0:T(8,128)(2,1)S(1)}, u32[]{:S(2)}, u32[]{:S(2)}) async-start(bf16[8,2,2,128,128]{4,3,2,1,0:T(8,128)(2,1)} %get-tuple-element.108), calls=%async_computation | async-start | bytes 2097152 | tf_op jit(solution)/shard_map/all_to_all | solution.py:528

commit v3 on v2

--- a/solution.py
+++ b/solution.py
@@ -577,6 +577,7 @@
     slots[1], side0, later_len = lax.optimization_barrier((slots[1], side0, group_len))
     side1 = sides(slots[1])
     scale = row_scales(later_len, place, hidden)
+    side0, side1 = lax.optimization_barrier((side0, side1))
     far = opposite(side0[0], side1[1])
     side1, scale, sibling = lax.optimization_barrier((side1, scale, sibling))
     other_scale = lax.ppermute(scale, "tp", swap)

time: 111 us -> 109 us (0.982); the launches traced: 111 us -> 110 us
  Pallas kernels: 32.4 us -> 25.9 us
  waiting for transfers between devices: 41.1 us -> 46.4 us
    pallas_call x2, Pallas kernels: 14.3 us -> 10.5 us  [project_near(): pl.pallas_call(functools.partial(near_kernel, tile, depth, pieces), in_sp...]
    ppermute x2, waiting for transfers between devices: 0.01 us -> 2.89 us  [opposite(): lax.ppermute(second_side1, 'grp', flip0)]
    pallas_call x2, Pallas kernels: 11.7 us -> 8.92 us  [project_far(): pl.pallas_call(functools.partial(far_kernel, slot_ids, tile, depth, deep)...]
    ppermute x1, waiting for transfers between devices: 0.62 us -> 3.05 us  [paired(): passed = lax.ppermute(across, 'tp', outward)]
    all_to_all x2, starting transfers between devices: 9.04 us -> 11.2 us  [exchange(): return lax.all_to_all(sent, 'tp', split_axis=0, concat_axis=0, tiled=True)]
    all_to_all x2, waiting for transfers between devices: 26.5 us -> 27.9 us  [exchange(): return lax.all_to_all(sent, 'tp', split_axis=0, concat_axis=0, tiled=True)]
    ppermute x2, starting transfers between devices: 2.9 us -> 1.62 us  [opposite(): lax.ppermute(second_side1, 'grp', flip0)]
  transfers between devices with their start and end apart: 18 -> 18, of which waited for: 8 -> 12; matrix products, arithmetic and copies ran while one was open for 6% -> 6% of each run, Pallas kernels for 28% -> 22%
where the time goes in v3:
time: 109 us; the launch traced here: 110 us
  waiting for transfers between devices  46.4 us (43%)
  starting transfers between devices  29.7 us (27%)
  Pallas kernels  25.9 us (24%)
  local copies, waits for them, and re-layouts  4.45 us (4%)
  other arithmetic  2.93 us (3%)
    all_to_all x2, waiting for transfers between devices, exchange(): return lax.all_to_all(sent, 'tp', split_axis=0, concat_axis=0, tiled=True)  27.9 us
    all_to_all x2, starting transfers between devices, exchange(): return lax.all_to_all(sent, 'tp', split_axis=0, concat_axis=0, tiled=True)  11.2 us
    pallas_call x2, Pallas kernels, project_near(): pl.pallas_call(functools.partial(near_kernel, tile, depth, pieces), in_sp...  10.5 us
    pallas_call x2, Pallas kernels, project_far(): pl.pallas_call(functools.partial(far_kernel, slot_ids, tile, depth, deep)...  8.92 us
    ppermute x3, waiting for transfers between devices, sides(): lax.ppermute(shard, 'grp', flip0)  4.33 us
    ppermute x3, waiting for transfers between devices, sides(): lax.ppermute(shard, 'grp', flip1)  4.29 us
    ppermute x1, waiting for transfers between devices, from_chip(): return lax.ppermute(own, 'tp', [(i, i ^ 2 * flip) for i in range(tp_count)])  3.91 us
    ppermute x3, starting transfers between devices, sides(): lax.ppermute(shard, 'grp', flip0)  3.24 us
  transfers between devices with their start and end apart: 18, of which 12 were waited for; matrix products, arithmetic and copies ran while one was open for 6% of the time, Pallas kernels for 22%

profile of v3, /device:TPU:0, one launch (start us, length us, event | category | flops | bytes accessed | tf_op | source)
XLA Modules:
  0.0 110.2 jit_solution(11042008310549418292)
XLA Ops:
  0.0 0.5 collective-permute-start.13
  0.5 0.8 dynamic_slice.3
  1.2 1.2 %multiply_convert_fusion.refs_4_ = bf16[1280,128]{1,0:T(8,128)(2,1)S(1)} fusion(bf16[1280,128]{1,0:T(8,128)(2,1)} %param.18, f32[1280]{0:T(1024)S(1)} %dynamic_slice.3), kind=kLoop, calls=%fused_computation.13 | loop fusion | flops 491520 | bytes 660480 | tf_op jit(solution)/shard_map/convert_element_type | solution.py:545
  2.4 2.6 %collective-permute-start.7 = (bf16[1280,128]{1,0:T(8,128)(2,1)S(1)}, bf16[1280,128]{1,0:T(8,128)(2,1)S(1)}, u32[]{:S(2)}, u32[]{:S(2)}) collective-permute-start(bf16[1280,128]{1,0:T(8,128)(2,1)S(1)} %multiply_convert_fusion.refs_4_), channel_id=1, source_target_pairs={{0,2},{1,3},{2,0},{3,1},{4,6},{5,7},{6,4},{7,5},{8,10},{9,11},{10,... | collective-permute-start | bytes 983048 | tf_op jit(solution)/shard_map/ppermute | solution.py:550
  5.1 1.4 %collective-permute-start.8 = (bf16[1280,128]{1,0:T(8,128)(2,1)S(1)}, bf16[1280,128]{1,0:T(8,128)(2,1)}, u32[]{:S(2)}, u32[]{:S(2)}) collective-permute-start(bf16[1280,128]{1,0:T(8,128)(2,1)S(1)} %multiply_convert_fusion.refs_4_), channel_id=1, source_target_pairs={{2,4},{3,5},{4,2},{5,3},{10,12},{11,13},{12,10},{13,11},{18,20},{1... | collective-permute-start | bytes 983048 | tf_op jit(solution)/shard_map/ppermute | solution.py:570
  6.5 1.5 %collective-permute-start.10 = (bf16[1280,128]{1,0:T(8,128)(2,1)S(1)}, bf16[1280,128]{1,0:T(8,128)(2,1)S(1)}, u32[]{:S(2)}, u32[]{:S(2)}) collective-permute-start(bf16[1280,128]{1,0:T(8,128)(2,1)S(1)} %multiply_convert_fusion.refs_4_), channel_id=1, source_target_pairs={{0,16},{8,24},{16,0},{24,8},{1,17},{9,25},{17,1},{25,9},{2,18},{10... | collective-permute-start | bytes 983048 | tf_op jit(solution)/shard_map/ppermute | solution.py:123
  8.0 1.5 %collective-permute-start.9 = (bf16[1280,128]{1,0:T(8,128)(2,1)S(1)}, bf16[1280,128]{1,0:T(8,128)(2,1)S(1)}, u32[]{:S(2)}, u32[]{:S(2)}) collective-permute-start(bf16[1280,128]{1,0:T(8,128)(2,1)S(1)} %multiply_convert_fusion.refs_4_), channel_id=1, source_target_pairs={{0,8},{8,0},{16,24},{24,16},{1,9},{9,1},{17,25},{25,17},{2,10},{10... | collective-permute-start | bytes 983048 | tf_op jit(solution)/shard_map/ppermute | solution.py:123
  9.5 0.1 pad_add_fusion.place_ref.refs_1_
  9.6 3.9 %collective-permute-done.7.refs_7_ = bf16[1280,128]{1,0:T(8,128)(2,1)S(1)} collective-permute-done((bf16[1280,128]{1,0:T(8,128)(2,1)S(1)}, bf16[1280,128]{1,0:T(8,128)(2,1)S(1)}, u32[]{:S(2)}, u32[]{:S(2)}) %collective-permute-start.7) | collective-permute-done | bytes 327712 | tf_op jit(solution)/shard_map/ppermute | solution.py:550
  13.5 2.8 %collective-permute-done.10.refs_6_ = bf16[1280,128]{1,0:T(8,128)(2,1)S(1)} collective-permute-done((bf16[1280,128]{1,0:T(8,128)(2,1)S(1)}, bf16[1280,128]{1,0:T(8,128)(2,1)S(1)}, u32[]{:S(2)}, u32[]{:S(2)}) %collective-permute-start.10) | collective-permute-done | bytes 327712 | tf_op jit(solution)/shard_map/ppermute | solution.py:123
  16.3 1.2 %collective-permute-done.9.refs_5_ = bf16[1280,128]{1,0:T(8,128)(2,1)S(1)} collective-permute-done((bf16[1280,128]{1,0:T(8,128)(2,1)S(1)}, bf16[1280,128]{1,0:T(8,128)(2,1)S(1)}, u32[]{:S(2)}, u32[]{:S(2)}) %collective-permute-start.9) | collective-permute-done | bytes 327712 | tf_op jit(solution)/shard_map/ppermute | solution.py:123
  17.6 1.5 %collective-permute-start.11 = (bf16[1280,128]{1,0:T(8,128)(2,1)S(1)}, bf16[1280,128]{1,0:T(8,128)(2,1)S(1)}, u32[]{:S(2)}, u32[]{:S(2)}) collective-permute-start(bf16[1280,128]{1,0:T(8,128)(2,1)S(1)} %collective-permute-done.7.refs_7_), channel_id=1, source_target_pairs={{0,8},{8,0},{16,24},{24,16},{1,9},{9,1},{17,25},{25,17},{2,10},{10... | collective-permute-start | bytes 983048 | tf_op jit(solution)/shard_map/ppermute | solution.py:123
  19.0 0.5 collective-permute-start.12
  19.6 2.5 %collective-permute-start.17 = (bf16[1280,128]{1,0:T(8,128)(2,1)S(1)}, bf16[1280,128]{1,0:T(8,128)(2,1)S(1)}, u32[]{:S(2)}, u32[]{:S(2)}) collective-permute-start(bf16[1280,128]{1,0:T(8,128)(2,1)S(1)} %broadcast_select_fusion.2), channel_id=1, source_target_pairs={{2,4},{3,5},{4,2},{5,3},{0,6},{1,7},{6,0},{7,1},{10,12},{11,13},{1... | collective-permute-start | bytes 983048 | tf_op jit(solution)/shard_map/ppermute | solution.py:573
  22.1 1.3 %collective-permute-start.18 = (bf16[1280,128]{1,0:T(8,128)(2,1)}, bf16[1280,128]{1,0:T(8,128)(2,1)S(1)}, u32[]{:S(2)}, u32[]{:S(2)}) collective-permute-start(bf16[1280,128]{1,0:T(8,128)(2,1)} %collective-permute-done.8), channel_id=1, source_target_pairs={{2,0},{3,1},{4,6},{5,7},{10,8},{11,9},{12,14},{13,15},{18,16},{19,... | collective-permute-start | bytes 983048 | tf_op jit(solution)/shard_map/ppermute | solution.py:574
  23.4 2.7 %row_scales.1.refs_9_ = f32[1152,128]{1,0:T(8,128)S(1)} custom-call(s32[8]{0:T(128)S(1)} %bitcast.23, s32[2]{0:T(128)S(1)} %pad_add_fusion.place_ref.refs_1_, bf16[1152,5120]{1,0:T(8,128)(2,1)} %refs_2_.7), custom_call_target="tpu_custom_call" | custom-call | flops 17694720 | bytes 11796480 | tf_op jit(solution)/shard_map/row_scales/pallas_call | solution.py:163
  26.1 0.1 collective-permute-done.11.refs_8_
  26.2 1.2 %collective-permute-done.12.refs_9_ = bf16[1280,128]{1,0:T(8,128)(2,1)S(1)} collective-permute-done((bf16[1280,128]{1,0:T(8,128)(2,1)S(1)}, bf16[1280,128]{1,0:T(8,128)(2,1)S(1)}, u32[]{:S(2)}, u32[]{:S(2)}) %collective-permute-start.12) | collective-permute-done | bytes 327712 | tf_op jit(solution)/shard_map/ppermute | solution.py:123
  27.4 1.1 collective-permute-start.14
  28.6 5.1 %project_near.2.refs_6_ = f32[2688,256]{1,0:T(8,128)S(1)} custom-call(s32[8]{0:T(128)S(1)} %bitcast.24, s32[2]{0:T(128)S(1)} %pad_add_fusion.place_ref.refs_1_, bf16[1152,5120]{1,0:T(8,128)(2,1)} %refs_2_.7, bf16[1152,5120]{1,0:T(8,128)(2,1)} %collective-permute-done.13.refs_3_, bf16[1280,128]{1,0:T(8,128)(2,1)S(1)} %multiply_convert_fusion.refs_4_, ...), custom_call_target="tpu_custom_call" | custom-call | flops 9059696640 | bytes 35389440 | tf_op jit(solution)/shard_map/project_near/pallas_call | solution.py:269
  33.7 3.0 %collective-permute-done.18 = bf16[1280,128]{1,0:T(8,128)(2,1)S(1)} collective-permute-done((bf16[1280,128]{1,0:T(8,128)(2,1)}, bf16[1280,128]{1,0:T(8,128)(2,1)S(1)}, u32[]{:S(2)}, u32[]{:S(2)}) %collective-permute-start.18) | collective-permute-done | bytes 327712 | tf_op jit(solution)/shard_map/ppermute | solution.py:574
  36.8 1.2 %collective-permute-done.15.refs_5_ = bf16[1280,128]{1,0:T(8,128)(2,1)S(1)} collective-permute-done((bf16[1280,128]{1,0:T(8,128)(2,1)S(1)}, bf16[1280,128]{1,0:T(8,128)(2,1)S(1)}, u32[]{:S(2)}, u32[]{:S(2)}) %collective-permute-start.15) | collective-permute-done | bytes 327712 | tf_op jit(solution)/shard_map/ppermute | solution.py:127
  38.0 0.1 broadcast_select_fusion.1
  38.1 0.9 pad_maximum_fusion.1.refs_4_
  39.0 0.3 collective-permute-start.19
  39.3 0.5 collective-permute-start.20
  39.8 4.5 %project_far.2 = (bf16[8,2,2,128,128]{4,3,2,1,0:T(8,128)(2,1)}, bf16[2,2,128,128]{3,2,1,0:T(8,128)(2,1)S(1)}) custom-call(s32[8]{0:T(128)S(1)} %bitcast.25, s32[2]{0:T(128)S(1)} %pad_add_fusion.place_ref.refs_1_, bf16[1152,5120]{1,0:T(8,128)(2,1)} %refs_2_.7, bf16[1152,5120]{1,0:T(8,128)(2,1)} %collective-permute-done.13.refs_3_, ...), custom_call_target="tpu_custom_call" | custom-call | flops 6039797760 | bytes 23592960 | tf_op jit(solution)/shard_map/project_far/pallas_call | solution.py:390
  44.2 7.7 %all-to-all-start.1 = ((bf16[8,2,2,128,128]{4,3,2,1,0:T(8,128)(2,1)}), bf16[8,2,2,128,128]{4,3,2,1,0:T(8,128)(2,1)S(1)}, u32[]{:S(2)}, u32[]{:S(2)}) async-start(bf16[8,2,2,128,128]{4,3,2,1,0:T(8,128)(2,1)} %get-tuple-element.117), calls=%async_computation.1 | async-start | bytes 2097152 | tf_op jit(solution)/shard_map/all_to_all | solution.py:528
  51.9 3.0 %collective-permute-done.19.refs_5_ = bf16[2560,128]{1,0:T(8,128)(2,1)} collective-permute-done((bf16[2560,128]{1,0:T(8,128)(2,1)}, bf16[2560,128]{1,0:T(8,128)(2,1)}, u32[]{:S(2)}, u32[]{:S(2)}) %collective-permute-start.19) | collective-permute-done | bytes 655392 | tf_op jit(solution)/shard_map/ppermute | solution.py:123
  54.9 0.2 collective-permute-done.20.refs_6_
  55.2 1.0 slice.38
  56.1 1.7 %collective-permute-start.21 = (bf16[1280,128]{1,0:T(8,128)(2,1)S(1)}, bf16[1280,128]{1,0:T(8,128)(2,1)S(1)}, u32[]{:S(2)}, u32[]{:S(2)}) collective-permute-start(bf16[1280,128]{1,0:T(8,128)(2,1)S(1)} %slice.38), channel_id=1, source_target_pairs={{0,16},{8,24},{16,0},{24,8},{1,17},{9,25},{17,1},{25,9},{2,18},{10... | collective-permute-start | bytes 983048 | tf_op jit(solution)/shard_map/ppermute | solution.py:127
  57.8 1.0 slice.39
  58.8 1.6 %collective-permute-start.22 = (bf16[1280,128]{1,0:T(8,128)(2,1)S(1)}, bf16[1280,128]{1,0:T(8,128)(2,1)S(1)}, u32[]{:S(2)}, u32[]{:S(2)}) collective-permute-start(bf16[1280,128]{1,0:T(8,128)(2,1)S(1)} %slice.39), channel_id=1, source_target_pairs={{0,8},{8,0},{16,24},{24,16},{1,9},{9,1},{17,25},{25,17},{2,10},{10... | collective-permute-start | bytes 983048 | tf_op jit(solution)/shard_map/ppermute | solution.py:127
  60.4 5.3 %project_near.3.refs_6_ = f32[2688,256]{1,0:T(8,128)S(1)} custom-call(s32[8]{0:T(128)S(1)} %bitcast.26, s32[2]{0:T(128)S(1)} %pad_add_fusion.place_ref.refs_1_, bf16[1152,5120]{1,0:T(8,128)(2,1)} %refs_2_.7, bf16[1152,5120]{1,0:T(8,128)(2,1)} %collective-permute-done.13.refs_3_, bf16[2560,128]{1,0:T(8,128)(2,1)} %pad_maximum_fusion.1.refs_4_, ...), custom_call_target="tpu_custom_call" | custom-call | flops 9059696640 | bytes 35389440 | tf_op jit(solution)/shard_map/project_near/pallas_call | solution.py:269
  65.7 1.7 %collective-permute-done.22.refs_5_ = bf16[1280,128]{1,0:T(8,128)(2,1)S(1)} collective-permute-done((bf16[1280,128]{1,0:T(8,128)(2,1)S(1)}, bf16[1280,128]{1,0:T(8,128)(2,1)S(1)}, u32[]{:S(2)}, u32[]{:S(2)}) %collective-permute-start.22) | collective-permute-done | bytes 327712 | tf_op jit(solution)/shard_map/ppermute | solution.py:127
  67.4 4.5 %project_far.3 = (bf16[8,2,2,128,128]{4,3,2,1,0:T(8,128)(2,1)}, bf16[2,2,128,128]{3,2,1,0:T(8,128)(2,1)}) custom-call(s32[8]{0:T(128)S(1)} %bitcast.27, s32[2]{0:T(128)S(1)} %pad_add_fusion.place_ref.refs_1_, bf16[1152,5120]{1,0:T(8,128)(2,1)} %refs_2_.7, bf16[1152,5120]{1,0:T(8,128)(2,1)} %collective-permute-done.13.refs_3_, ...), custom_call_target="tpu_custom_call" | custom-call | flops 6039797760 | bytes 23592960 | tf_op jit(solution)/shard_map/project_far/pallas_call | solution.py:390
  71.9 6.6 %all-to-all-done.1.refs_0_ = bf16[8,2,2,128,128]{4,3,2,1,0:T(8,128)(2,1)S(1)} async-done(((bf16[8,2,2,128,128]{4,3,2,1,0:T(8,128)(2,1)}), bf16[8,2,2,128,128]{4,3,2,1,0:T(8,128)(2,1)S(1)}, u32[]{:S(2)}, u32[]{:S(2)}) %all-to-all-start.1) | async-done | bytes 1048608 | tf_op jit(solution)/shard_map/all_to_all | solution.py:528
  78.5 3.6 %all-to-all-start = ((bf16[8,2,2,128,128]{4,3,2,1,0:T(8,128)(2,1)}), bf16[8,2,2,128,128]{4,3,2,1,0:T(8,128)(2,1)S(1)}, u32[]{:S(2)}, u32[]{:S(2)}) async-start(bf16[8,2,2,128,128]{4,3,2,1,0:T(8,128)(2,1)} %get-tuple-element.116), calls=%async_computation | async-start | bytes 2097152 | tf_op jit(solution)/shard_map/all_to_all | solution.py:528
  82.1 0.1 slice.40
  82.2 0.1 slice.41
  82.3 0.6 fusion.1
  83.6 1.5 %conditional.3 = (bf16[2,4,128,128]{3,2,1,0:T(8,128)(2,1)}, bf16[2,4,128,128]{3,2,1,0:T(8,128)(2,1)}) conditional(s32[]{:T(128)} %convert_element_type.11, () %tuple.61, (s32[]{:T(128)}, s32[4]{0:T(128)S(1)}, bf16[2,2,128,128]{3,2,1,0:T(8,128)(2,1)S(1)}, bf16[2,2,128,128]{3,2,1,0:T(8,128)(2,1)S(1)}) %tuple.75), branch_computations={%region_1.2_spmd, %region_2.13_spmd} | conditional | flops 131166 | bytes 3670858 | solution.py:626
  83.6 0.7 broadcast.21
  84.3 0.7 broadcast.21.clone
  85.1 2.2 %assemble_early.1.base_ref = bf16[5,128,1024]{2,1,0:T(8,128)(2,1)} custom-call(s32[8]{0:T(128)S(1)} %bitcast.28, s32[2]{0:T(128)S(1)} %pad_add_fusion.place_ref.refs_1_, bf16[8,2,2,128,128]{4,3,2,1,0:T(8,128)(2,1)S(1)} %all-to-all-done.1.refs_0_, bf16[2,4,128,128]{3,2,1,0:T(8,128)(2,1)} %get-tuple-element.120.refs_1_, ...), custom_call_target="tpu_custom_call" | custom-call | tf_op jit(solution)/shard_map/assemble_early/pallas_call | solution.py:472
  87.3 21.3 %all-to-all-done.arrived = bf16[8,2,2,128,128]{4,3,2,1,0:T(8,128)(2,1)S(1)} async-done(((bf16[8,2,2,128,128]{4,3,2,1,0:T(8,128)(2,1)}), bf16[8,2,2,128,128]{4,3,2,1,0:T(8,128)(2,1)S(1)}, u32[]{:S(2)}, u32[]{:S(2)}) %all-to-all-start) | async-done | bytes 1048608 | tf_op jit(solution)/shard_map/all_to_all | solution.py:528
  108.6 1.6 %assemble_late.1 = bf16[5,128,1024]{2,1,0:T(8,128)(2,1)} custom-call(s32[8]{0:T(128)S(1)} %bitcast.29, s32[2]{0:T(128)S(1)} %pad_add_fusion.place_ref.refs_1_, bf16[8,2,2,128,128]{4,3,2,1,0:T(8,128)(2,1)S(1)} %all-to-all-done.arrived, bf16[5,128,1024]{2,1,0:T(8,128)(2,1)} %assemble_early.1.base_ref), custom_call_target="tpu_custom_call", output_to_operand_aliasing={{}: (3, {})} | custom-call | tf_op jit(solution)/shard_map/assemble_late/pallas_call | solution.py:508
  (18 shorter events, 0.2 us)
Async XLA Ops:
  0.0 23.4 %copy-start.1 = (s32[1,8]{1,0:T(1,128)S(1)}, s32[1,8]{1,0:T(1,128)}, u32[]{:S(2)}) copy-start(s32[1,8]{1,0:T(1,128)} %param.17) | copy-start | bytes 100
  0.0 28.6 %collective-permute-start.13 = (bf16[1152,5120]{1,0:T(8,128)(2,1)}, bf16[1152,5120]{1,0:T(8,128)(2,1)}, u32[]{:S(2)}, u32[]{:S(2)}) collective-permute-start(bf16[1152,5120]{1,0:T(8,128)(2,1)} %refs_2_.7), channel_id=1, source_target_pairs={{0,1},{1,0},{2,3},{3,2},{4,5},{5,4},{6,7},{7,6},{8,9},{9,8},{10,11... | collective-permute-start | bytes 35389448 | tf_op jit(solution)/shard_map/ppermute | solution.py:546
  2.4 11.0 %collective-permute-start.7 = (bf16[1280,128]{1,0:T(8,128)(2,1)S(1)}, bf16[1280,128]{1,0:T(8,128)(2,1)S(1)}, u32[]{:S(2)}, u32[]{:S(2)}) collective-permute-start(bf16[1280,128]{1,0:T(8,128)(2,1)S(1)} %multiply_convert_fusion.refs_4_), channel_id=1, source_target_pairs={{0,2},{1,3},{2,0},{3,1},{4,6},{5,7},{6,4},{7,5},{8,10},{9,11},{10,... | collective-permute-start | bytes 983048 | tf_op jit(solution)/shard_map/ppermute | solution.py:550
  5.1 8.4 %collective-permute-start.8 = (bf16[1280,128]{1,0:T(8,128)(2,1)S(1)}, bf16[1280,128]{1,0:T(8,128)(2,1)}, u32[]{:S(2)}, u32[]{:S(2)}) collective-permute-start(bf16[1280,128]{1,0:T(8,128)(2,1)S(1)} %multiply_convert_fusion.refs_4_), channel_id=1, source_target_pairs={{2,4},{3,5},{4,2},{5,3},{10,12},{11,13},{12,10},{13,11},{18,20},{1... | collective-permute-start | bytes 983048 | tf_op jit(solution)/shard_map/ppermute | solution.py:570
  6.5 9.8 %collective-permute-start.10 = (bf16[1280,128]{1,0:T(8,128)(2,1)S(1)}, bf16[1280,128]{1,0:T(8,128)(2,1)S(1)}, u32[]{:S(2)}, u32[]{:S(2)}) collective-permute-start(bf16[1280,128]{1,0:T(8,128)(2,1)S(1)} %multiply_convert_fusion.refs_4_), channel_id=1, source_target_pairs={{0,16},{8,24},{16,0},{24,8},{1,17},{9,25},{17,1},{25,9},{2,18},{10... | collective-permute-start | bytes 983048 | tf_op jit(solution)/shard_map/ppermute | solution.py:123
  8.0 9.6 %collective-permute-start.9 = (bf16[1280,128]{1,0:T(8,128)(2,1)S(1)}, bf16[1280,128]{1,0:T(8,128)(2,1)S(1)}, u32[]{:S(2)}, u32[]{:S(2)}) collective-permute-start(bf16[1280,128]{1,0:T(8,128)(2,1)S(1)} %multiply_convert_fusion.refs_4_), channel_id=1, source_target_pairs={{0,8},{8,0},{16,24},{24,16},{1,9},{9,1},{17,25},{25,17},{2,10},{10... | collective-permute-start | bytes 983048 | tf_op jit(solution)/shard_map/ppermute | solution.py:123
  17.6 8.7 %collective-permute-start.11 = (bf16[1280,128]{1,0:T(8,128)(2,1)S(1)}, bf16[1280,128]{1,0:T(8,128)(2,1)S(1)}, u32[]{:S(2)}, u32[]{:S(2)}) collective-permute-start(bf16[1280,128]{1,0:T(8,128)(2,1)S(1)} %collective-permute-done.7.refs_7_), channel_id=1, source_target_pairs={{0,8},{8,0},{16,24},{24,16},{1,9},{9,1},{17,25},{25,17},{2,10},{10... | collective-permute-start | bytes 983048 | tf_op jit(solution)/shard_map/ppermute | solution.py:123
  19.0 8.4 %collective-permute-start.12 = (bf16[1280,128]{1,0:T(8,128)(2,1)S(1)}, bf16[1280,128]{1,0:T(8,128)(2,1)S(1)}, u32[]{:S(2)}, u32[]{:S(2)}) collective-permute-start(bf16[1280,128]{1,0:T(8,128)(2,1)S(1)} %collective-permute-done.7.refs_7_), channel_id=1, source_target_pairs={{0,16},{8,24},{16,0},{24,8},{1,17},{9,25},{17,1},{25,9},{2,18},{10... | collective-permute-start | bytes 983048 | tf_op jit(solution)/shard_map/ppermute | solution.py:123
  19.6 14.1 %collective-permute-start.17 = (bf16[1280,128]{1,0:T(8,128)(2,1)S(1)}, bf16[1280,128]{1,0:T(8,128)(2,1)S(1)}, u32[]{:S(2)}, u32[]{:S(2)}) collective-permute-start(bf16[1280,128]{1,0:T(8,128)(2,1)S(1)} %broadcast_select_fusion.2), channel_id=1, source_target_pairs={{2,4},{3,5},{4,2},{5,3},{0,6},{1,7},{6,0},{7,1},{10,12},{11,13},{1... | collective-permute-start | bytes 983048 | tf_op jit(solution)/shard_map/ppermute | solution.py:573
  22.1 14.7 %collective-permute-start.18 = (bf16[1280,128]{1,0:T(8,128)(2,1)}, bf16[1280,128]{1,0:T(8,128)(2,1)S(1)}, u32[]{:S(2)}, u32[]{:S(2)}) collective-permute-start(bf16[1280,128]{1,0:T(8,128)(2,1)} %collective-permute-done.8), channel_id=1, source_target_pairs={{2,0},{3,1},{4,6},{5,7},{10,8},{11,9},{12,14},{13,15},{18,16},{19,... | collective-permute-start | bytes 983048 | tf_op jit(solution)/shard_map/ppermute | solution.py:574
  27.4 9.3 %collective-permute-start.14 = (bf16[1280,128]{1,0:T(8,128)(2,1)S(1)}, bf16[1280,128]{1,0:T(8,128)(2,1)S(1)}, u32[]{:S(2)}, u32[]{:S(2)}) collective-permute-start(bf16[1280,128]{1,0:T(8,128)(2,1)S(1)} %collective-permute-done.9.refs_5_), channel_id=1, source_target_pairs={{0,16},{8,24},{16,0},{24,8},{1,17},{9,25},{17,1},{25,9},{2,18},{10... | collective-permute-start | bytes 983048 | tf_op jit(solution)/shard_map/ppermute | solution.py:127
  28.5 9.5 %collective-permute-start.15 = (bf16[1280,128]{1,0:T(8,128)(2,1)S(1)}, bf16[1280,128]{1,0:T(8,128)(2,1)S(1)}, u32[]{:S(2)}, u32[]{:S(2)}) collective-permute-start(bf16[1280,128]{1,0:T(8,128)(2,1)S(1)} %collective-permute-done.12.refs_9_), channel_id=1, source_target_pairs={{0,8},{8,0},{16,24},{24,16},{1,9},{9,1},{17,25},{25,17},{2,10},{10... | collective-permute-start | bytes 983048 | tf_op jit(solution)/shard_map/ppermute | solution.py:127
  28.6 9.4 %collective-permute-start.16 = (f32[1152,128]{1,0:T(8,128)S(1)}, f32[1152,128]{1,0:T(8,128)S(1)}, u32[]{:S(2)}, u32[]{:S(2)}) collective-permute-start(f32[1152,128]{1,0:T(8,128)S(1)} %row_scales.1.refs_9_), channel_id=1, source_target_pairs={{0,1},{1,0},{2,3},{3,2},{4,5},{5,4},{6,7},{7,6},{8,9},{9,8},{10,11... | collective-permute-start | bytes 1769480 | tf_op jit(solution)/shard_map/ppermute | solution.py:583
  33.7 6.0 %copy-start = (f32[1152,256]{1,0:T(8,128)S(1)}, f32[1152,256]{1,0:T(8,128)}, u32[]{:S(2)}) copy-start(f32[1152,256]{1,0:T(8,128)} %constant.100.clone.refs_7_) | copy-start | bytes 3538948
  33.7 6.0 %copy-start.2 = (f32[128]{0:T(128)S(1)}, f32[128]{0:T(128)}, u32[]{:S(2)}) copy-start(f32[128]{0:T(128)} %param.20) | copy-start | bytes 1540
  39.0 15.9 %collective-permute-start.19 = (bf16[2560,128]{1,0:T(8,128)(2,1)}, bf16[2560,128]{1,0:T(8,128)(2,1)}, u32[]{:S(2)}, u32[]{:S(2)}) collective-permute-start(bf16[2560,128]{1,0:T(8,128)(2,1)} %pad_maximum_fusion.1.refs_4_), channel_id=1, source_target_pairs={{0,8},{8,0},{16,24},{24,16},{1,9},{9,1},{17,25},{25,17},{2,10},{10... | collective-permute-start | bytes 1966088 | tf_op jit(solution)/shard_map/ppermute | solution.py:123
  39.3 15.9 %collective-permute-start.20 = (bf16[2560,128]{1,0:T(8,128)(2,1)}, bf16[2560,128]{1,0:T(8,128)(2,1)}, u32[]{:S(2)}, u32[]{:S(2)}) collective-permute-start(bf16[2560,128]{1,0:T(8,128)(2,1)} %pad_maximum_fusion.1.refs_4_), channel_id=1, source_target_pairs={{0,16},{8,24},{16,0},{24,8},{1,17},{9,25},{17,1},{25,9},{2,18},{10... | collective-permute-start | bytes 1966088 | tf_op jit(solution)/shard_map/ppermute | solution.py:123
  44.2 34.3 %all-to-all-start.1 = ((bf16[8,2,2,128,128]{4,3,2,1,0:T(8,128)(2,1)}), bf16[8,2,2,128,128]{4,3,2,1,0:T(8,128)(2,1)S(1)}, u32[]{:S(2)}, u32[]{:S(2)}) async-start(bf16[8,2,2,128,128]{4,3,2,1,0:T(8,128)(2,1)} %get-tuple-element.117), calls=%async_computation.1 | async-start | bytes 2097152 | tf_op jit(solution)/shard_map/all_to_all | solution.py:528
  56.1 9.6 %collective-permute-start.21 = (bf16[1280,128]{1,0:T(8,128)(2,1)S(1)}, bf16[1280,128]{1,0:T(8,128)(2,1)S(1)}, u32[]{:S(2)}, u32[]{:S(2)}) collective-permute-start(bf16[1280,128]{1,0:T(8,128)(2,1)S(1)} %slice.38), channel_id=1, source_target_pairs={{0,16},{8,24},{16,0},{24,8},{1,17},{9,25},{17,1},{25,9},{2,18},{10... | collective-permute-start | bytes 983048 | tf_op jit(solution)/shard_map/ppermute | solution.py:127
  58.8 8.6 %collective-permute-start.22 = (bf16[1280,128]{1,0:T(8,128)(2,1)S(1)}, bf16[1280,128]{1,0:T(8,128)(2,1)S(1)}, u32[]{:S(2)}, u32[]{:S(2)}) collective-permute-start(bf16[1280,128]{1,0:T(8,128)(2,1)S(1)} %slice.39), channel_id=1, source_target_pairs={{0,8},{8,0},{16,24},{24,16},{1,9},{9,1},{17,25},{25,17},{2,10},{10... | collective-permute-start | bytes 983048 | tf_op jit(solution)/shard_map/ppermute | solution.py:127
  71.9 11.7 %copy-start.3 = (bf16[2,2,128,128]{3,2,1,0:T(8,128)(2,1)S(1)}, bf16[2,2,128,128]{3,2,1,0:T(8,128)(2,1)}, u32[]{:S(2)}) copy-start(bf16[2,2,128,128]{3,2,1,0:T(8,128)(2,1)} %get-tuple-element.119) | copy-start | bytes 393220
  78.5 30.1 %all-to-all-start = ((bf16[8,2,2,128,128]{4,3,2,1,0:T(8,128)(2,1)}), bf16[8,2,2,128,128]{4,3,2,1,0:T(8,128)(2,1)S(1)}, u32[]{:S(2)}, u32[]{:S(2)}) async-start(bf16[8,2,2,128,128]{4,3,2,1,0:T(8,128)(2,1)} %get-tuple-element.116), calls=%async_computation | async-start | bytes 2097152 | tf_op jit(solution)/shard_map/all_to_all | solution.py:528
